TPU v7x, 128 devices: a whole 4x4x4 slice. The times are simulated.
128 devices in a mesh: gx: 4 (over y), gy: 4 (over z_lo, core), gz: 8 (over z_hi, x).
Axes of the slice: x: 4, y: 4, z: 4 (z_hi: 2, z_lo: 2; z = z_hi * 2 + z_lo), core: 2. Of those that a mesh axis runs over, the one named last changes fastest.
Arguments:
- positions: float32 [3, 16384], P(None, ('gx', 'gy', 'gz')), may hold values from -8 to 8
- atom_features: float32 [16384, 128], P(('gx', 'gy', 'gz')), may hold values from -6 to 6
- send_face: int32 [128, 6, 32], P(('gx', 'gy', 'gz')), may hold values from 0 to 127
- send_edge: int32 [128, 12, 8], P(('gx', 'gy', 'gz')), may hold values from 0 to 127
- send_corner: int32 [128, 8, 2], P(('gx', 'gy', 'gz')), may hold values from 0 to 127
- centre: int32 [786432], P(('gx', 'gy', 'gz')), may hold values from 0 to 127
- other: int32 [786432], P(('gx', 'gy', 'gz')), may hold values from 0 to 431
- edge_count: int32 [128], P(('gx', 'gy', 'gz')), may hold values from 1536 to 6144, as said below
- w_proj_a: float32 [128, 128], replicated, may hold values from -0.5 to 0.5
- w_proj_b: float32 [128, 128], replicated, may hold values from -0.5 to 0.5
- w_radial: float32 [8, 128], replicated, may hold values from -2 to 2
- w_first: bfloat16 [128, 128], replicated, may hold values from -0.5 to 0.5
- w_env: bfloat16 [128, 128], replicated, may hold values from -0.5 to 0.5
- w_value: bfloat16 [128, 128], replicated, may hold values from -0.5 to 0.5
- w_second: bfloat16 [256, 128], replicated, may hold values from -0.375 to 0.375
- w_out: bfloat16 [128], replicated, may hold values from -0.5 to 0.5
Outputs:
- forces: float32 [3, 16384], P(None, ('gx', 'gy', 'gz'))
- atom_energy: float32 [16384], P(('gx', 'gy', 'gz'))
- feature_grad: float32 [16384, 128], P(('gx', 'gy', 'gz'))
Inputs may be any that keep to these rules, and one draw needn't show every extreme that they name: `edge_count`: some domain has exactly 6144 live edges in every draw.
All inputs are finite; a program needn't handle non-finite values.
Results may differ from a plain program's by a relative error of at most 0.035.
Values sent between devices are 32-bit elements; how exact they have to be, the bound alone decides.
A program may use at most 192 MiB of HBM per device.

v0:
```python
import math

import jax
import jax.numpy as jnp
import numpy as np
from jax import lax
from jax.sharding import PartitionSpec as P


def padded(cells, sides, width):
    for axis, dim in sides:
        count = lax.axis_size(axis)
        head = lax.slice_in_dim(cells, 0, width, axis=dim)
        tail = lax.slice_in_dim(cells, cells.shape[dim] - width, cells.shape[dim], axis=dim)
        cells = jnp.concatenate(
            [
                lax.ppermute(tail, axis, [(i, (i + 1) % count) for i in range(count)]),
                cells,
                lax.ppermute(head, axis, [((i + 1) % count, i) for i in range(count)]),
            ],
            axis=dim,
        )
    return cells


def offsets_table():
    rows = []
    for a in (-1, 0, 1):
        for b in (-1, 0, 1):
            for c in (-1, 0, 1):
                if a != 0 or b != 0 or c != 0:
                    rows.append((a, b, c))
    return np.array(rows, dtype=np.int32)


def class_keys():
    groups = [[], [], []]
    index = 0
    for a in (-1, 0, 1):
        for b in (-1, 0, 1):
            for c in (-1, 0, 1):
                if a != 0 or b != 0 or c != 0:
                    groups[abs(a) + abs(b) + abs(c) - 1].append(index)
                    index = index + 1
    return [np.array(group, dtype=np.int32) for group in groups]


def harmonics(unit):
    ux, uy, uz = (unit[0], unit[1], unit[2])
    return [
        jnp.ones_like(ux),
        ux,
        uy,
        uz,
        1.732 * ux * uy,
        1.732 * uy * uz,
        1.732 * ux * uz,
        0.866 * (ux * ux - uy * uy),
        0.5 * (3.0 * uz * uz - 1.0),
    ]


def local_energy(
    pos_tab,
    proj_a,
    proj_b,
    centre,
    other,
    valid,
    w_radial,
    w_first,
    w_env,
    w_value,
    w_second,
    w_out,
):
    n_own = proj_a.shape[0]
    disp = jnp.take(pos_tab, other, axis=1) - jnp.take(pos_tab, centre, axis=1)
    dist = jnp.sqrt(jnp.sum(disp * disp, axis=0) + 0.01)
    unit = disp / dist[None, :]
    envelope = 1.0 / (1.0 + (dist / 2.0) ** 2) ** 2
    orders = jnp.arange(1, w_radial.shape[0] + 1).astype(jnp.float32)
    basis = (
        jnp.sin(orders[None, :] * (math.pi / 2.0) * dist[:, None])
        / dist[:, None]
        * envelope[:, None]
    )
    radial = jnp.dot(basis, w_radial, precision=lax.Precision.HIGHEST)
    mixed = (jnp.take(proj_a, centre, axis=0) + jnp.take(proj_b, other, axis=0) + radial).astype(
        jnp.bfloat16
    )
    first = jax.nn.silu(jnp.dot(mixed, w_first, preferred_element_type=jnp.float32)).astype(
        jnp.bfloat16
    )
    env_weight = (
        jnp.dot(first, w_env, preferred_element_type=jnp.float32) * (envelope * valid)[:, None]
    )
    value = jnp.dot(first, w_value, preferred_element_type=jnp.float32)
    total = jnp.zeros(value.shape, jnp.float32)
    for comp in harmonics(unit):
        env_m = jax.ops.segment_sum(env_weight * comp[:, None], centre, num_segments=n_own)
        total = total + comp[:, None] * jnp.take(env_m, centre, axis=0)
    scalar = (0.2 * value * total).astype(jnp.bfloat16)
    joined = jnp.concatenate([first, scalar], axis=1)
    second = jax.nn.silu(jnp.dot(joined, w_second, preferred_element_type=jnp.float32)).astype(
        jnp.bfloat16
    )
    edge_energy = jnp.dot(second, w_out, preferred_element_type=jnp.float32) * envelope * valid
    atom_energy = jax.ops.segment_sum(edge_energy, centre, num_segments=n_own)
    return (jnp.sum(edge_energy), atom_energy)


def place(items):
    blank = jnp.zeros_like(items[:1])
    return jnp.concatenate([items[:13], blank, items[13:]], axis=0).reshape(
        (3, 3, 3) + items.shape[1:]
    )


def place_back(items):
    slots = place(items).reshape((27,) + items.shape[1:])
    return slots[::-1].reshape((3, 3, 3) + items.shape[1:])


def pick(extended, flat_index):
    merged = extended.reshape((125,) + extended.shape[3:])
    return jnp.take(merged, jnp.asarray(flat_index), axis=0)


def lift(items, keys):
    full = jnp.zeros((26,) + items.shape[1:], items.dtype)
    return full.at[jnp.asarray(keys)].set(items)


def widen(items, axis, width):
    extra = width - items.shape[axis]
    pads = [(0, 0)] * items.ndim
    pads[axis] = (0, extra)
    return jnp.pad(items, pads)


def local(
    positions,
    atom_features,
    send_face,
    send_edge,
    send_corner,
    centre,
    other,
    edge_count,
    w_proj_a,
    w_proj_b,
    w_radial,
    w_first,
    w_env,
    w_value,
    w_second,
    w_out,
):
    high = lax.Precision.HIGHEST
    n_own = positions.shape[1]
    chans = atom_features.shape[1]
    keys_all = class_keys()
    lists_all = [send_face[0], send_edge[0], send_corner[0]]
    widths = [lists.shape[1] for lists in lists_all]
    widest = widths[0]
    flat_all = jnp.concatenate([lists.reshape(-1) for lists in lists_all], axis=0)
    offs = offsets_table()
    incoming = (2 - 2 * offs[:, 0]) * 25 + (2 - 2 * offs[:, 1]) * 5 + (2 - 2 * offs[:, 2])
    outgoing = (2 + 2 * offs[:, 0]) * 25 + (2 + 2 * offs[:, 1]) * 5 + (2 + 2 * offs[:, 2])
    proj_a = jnp.dot(atom_features, w_proj_a, precision=high)
    send_rows = []
    send_pos = []
    for keys, lists, width in zip(keys_all, lists_all, widths):
        flat_list = lists.reshape(-1)
        send_rows.append(
            jnp.take(atom_features, flat_list, axis=0).reshape(keys.shape[0], width, chans)
        )
        send_pos.append(
            jnp.transpose(
                jnp.take(positions, flat_list, axis=1).reshape(3, keys.shape[0], width), (1, 0, 2)
            )
        )
    recv_rows = []
    recv_pos = []
    full_rows = sum((lift(widen(r, 1, widest), k) for r, k in zip(send_rows, keys_all)))
    full_pos = sum((lift(widen(p, 2, widest), k) for p, k in zip(send_pos, keys_all)))
    ext_rows, ext_pos = (
        padded(place(full_rows), (("gx", 0), ("gy", 1), ("gz", 2)), 1),
        padded(place(full_pos), (("gx", 0), ("gy", 1), ("gz", 2)), 1),
    )
    all_rows = pick(ext_rows, incoming)
    all_pos = pick(ext_pos, incoming)
    for keys, width in zip(keys_all, widths):
        recv_rows.append(all_rows[keys][:, :width])
        recv_pos.append(all_pos[keys][:, :, :width])
    ghost_rows = jnp.concatenate([r.reshape(-1, chans) for r in recv_rows], axis=0)
    ghost_pos = jnp.concatenate(
        [jnp.transpose(p, (1, 0, 2)).reshape(3, -1) for p in recv_pos], axis=1
    )
    pos_tab = jnp.concatenate([positions, ghost_pos], axis=1)
    own_b = jnp.dot(atom_features, w_proj_b, precision=high)
    proj_tab = jnp.concatenate([own_b, jnp.dot(ghost_rows, w_proj_b, precision=high)], axis=0)
    valid = (jnp.arange(centre.shape[0]) < edge_count[0]).astype(jnp.float32)

    def energy(p, a, b):
        return local_energy(
            p, a, b, centre, other, valid, w_radial, w_first, w_env, w_value, w_second, w_out
        )

    total, pullback, atom_energy = jax.vjp(energy, pos_tab, proj_a, proj_tab, has_aux=True)
    grad_pos, grad_a, grad_b = pullback(jnp.ones((), jnp.float32))
    ghost_grad = jnp.dot(grad_b[n_own:], w_proj_b.T, precision=high)
    back_rows = []
    back_pos = []
    start = 0
    for keys, width in zip(keys_all, widths):
        count = keys.shape[0] * width
        back_rows.append(ghost_grad[start : start + count].reshape(keys.shape[0], width, chans))
        back_pos.append(
            jnp.transpose(
                grad_pos[:, n_own + start : n_own + start + count].reshape(3, keys.shape[0], width),
                (1, 0, 2),
            )
        )
        start = start + count
    got_rows = []
    got_pos = []
    full_rows = sum((lift(widen(r, 1, widest), k) for r, k in zip(back_rows, keys_all)))
    full_pos = sum((lift(widen(p, 2, widest), k) for p, k in zip(back_pos, keys_all)))
    ret_rows, ret_pos = (
        padded(place_back(full_rows), (("gx", 0), ("gy", 1), ("gz", 2)), 1),
        padded(place_back(full_pos), (("gx", 0), ("gy", 1), ("gz", 2)), 1),
    )
    all_rows = pick(ret_rows, outgoing)
    all_pos = pick(ret_pos, outgoing)
    for keys, width in zip(keys_all, widths):
        got_rows.append(all_rows[keys][:, :width])
        got_pos.append(all_pos[keys][:, :, :width])
    returned_rows = jnp.concatenate([r.reshape(-1, chans) for r in got_rows], axis=0)
    returned_pos = jnp.concatenate(
        [jnp.transpose(p, (0, 2, 1)).reshape(-1, 3) for p in got_pos], axis=0
    )
    force_sum = (
        grad_pos[:, :n_own] + jax.ops.segment_sum(returned_pos, flat_all, num_segments=n_own).T
    )
    added_rows = jax.ops.segment_sum(returned_rows, flat_all, num_segments=n_own)
    feature_grad = (
        jnp.dot(grad_a, w_proj_a.T, precision=high)
        + jnp.dot(grad_b[:n_own], w_proj_b.T, precision=high)
        + added_rows
    )
    return (-force_sum, atom_energy, feature_grad)


def solution(mesh):
    return jax.shard_map(
        local,
        mesh=mesh,
        in_specs=(
            P(None, ("gx", "gy", "gz")),
            P(("gx", "gy", "gz"), None),
            P(("gx", "gy", "gz"), None, None),
            P(("gx", "gy", "gz"), None, None),
            P(("gx", "gy", "gz"), None, None),
            P(("gx", "gy", "gz")),
            P(("gx", "gy", "gz")),
            P(("gx", "gy", "gz")),
            P(),
            P(),
            P(),
            P(),
            P(),
            P(),
            P(),
            P(),
        ),
        out_specs=(P(None, ("gx", "gy", "gz")), P(("gx", "gy", "gz")), P(("gx", "gy", "gz"), None)),
        check_vma=False,
    )
```

profile of v0, /device:TPU:1, one launch (start us, length us, event | category | flops | bytes accessed | tf_op | source)
XLA Modules:
  0.0 1527.7 jit_solution(16816413368297028495)
XLA Ops:
  47.8 16.1 %gather_fusion.30 = f32[6144,128]{1,0:T(8,128)S(1)} fusion(f32[128,128]{1,0:T(8,128)S(1)} %fusion.145, s32[6144]{0:T(1024)S(1)} %get-tuple-element.176), kind=kCustom, calls=%fused_computation.2.clone | custom fusion | bytes 6316032 | tf_op jit(solution)/shard_map/jvp(jit(_take))/gather | solution.py:89
  71.2 21.0 %gather_fusion.32 = f32[6144,3]{1,0:T(8,128)} fusion(f32[3,432]{0,1:T(8,128)S(1)} %copy.435, s32[6144]{0:T(1024)S(1)} %get-tuple-element.167), kind=kCustom, calls=%fused_computation.5.clone | custom fusion | bytes 172032 | tf_op jit(solution)/shard_map/jvp(jit(_take))/gather | solution.py:78
  95.2 21.0 %gather_fusion.29 = f32[6144,3]{1,0:T(8,128)} fusion(f32[3,432]{0,1:T(8,128)S(1)} %copy.435, s32[6144]{0:T(1024)S(1)} %copy-done.68), kind=kCustom, calls=%fused_computation.1.clone | custom fusion | bytes 172032 | tf_op jit(solution)/shard_map/jvp(jit(_take))/gather | solution.py:78
  158.1 23.2 %gather_fusion.12 = f32[6144,128]{1,0:T(8,128)} fusion(f32[432,128]{1,0:T(8,128)S(1)} %pad_maximum_fusion.22, s32[6144]{0:T(1024)} %copy-done.41), kind=kCustom, calls=%fused_computation.28 | custom fusion | bytes 6316032 | tf_op jit(solution)/shard_map/jvp(jit(_take))/gather | solution.py:89
  181.4 10.8 fusion
  203.2 33.5 %scatter_custom_fusion.7 = f32[128,128]{1,0:T(8,128)S(1)} fusion(s32[6144]{0:T(1024)} %param.46, f32[6144,128]{1,0:T(8,128)} %copy.441, f32[]{:T(128)} %constant.138.clone.1), kind=kCustom, calls=%fused_computation.300 | custom fusion | flops 786432 | bytes 66048 | tf_op jit(solution)/shard_map/jvp()/scatter-add | solution.py:101
  236.6 20.9 %gather_fusion.34 = f32[6144,128]{1,0:T(8,128)} fusion(f32[128,128]{1,0:T(8,128)S(1)} %scatter_custom_fusion.7, s32[6144]{0:T(1024)S(1)} %get-tuple-element.176), kind=kCustom, calls=%fused_computation.7.clone | custom fusion | bytes 6316032 | tf_op jit(solution)/shard_map/jvp(jit(_take))/gather | solution.py:102
  263.5 34.0 %scatter_custom_fusion.6 = f32[128,128]{1,0:T(8,128)S(1)} fusion(s32[6144]{0:T(1024)} %param.46, f32[6144,128]{1,0:T(8,128)} %copy.439, f32[]{:T(128)} %constant.138.clone.1), kind=kCustom, calls=%fused_computation.302 | custom fusion | flops 786432 | bytes 66048 | tf_op jit(solution)/shard_map/jvp()/scatter-add | solution.py:101
  297.6 20.9 %gather_fusion.33 = f32[6144,128]{1,0:T(8,128)} fusion(f32[128,128]{1,0:T(8,128)S(1)} %scatter_custom_fusion.6, s32[6144]{0:T(1024)S(1)} %get-tuple-element.176), kind=kCustom, calls=%fused_computation.6.clone | custom fusion | bytes 6316032 | tf_op jit(solution)/shard_map/jvp(jit(_take))/gather | solution.py:102
  332.3 33.4 %scatter_custom_fusion.8 = f32[128,128]{1,0:T(8,128)S(1)} fusion(s32[6144]{0:T(1024)} %param.46, f32[6144,128]{1,0:T(8,128)S(1)} %copy.443, f32[]{:T(128)} %constant.138.clone.1), kind=kCustom, calls=%fused_computation.298 | custom fusion | flops 786432 | bytes 66048 | tf_op jit(solution)/shard_map/jvp()/scatter-add | solution.py:101
  365.7 16.1 %gather_fusion.35 = f32[6144,128]{1,0:T(8,128)S(1)} fusion(f32[128,128]{1,0:T(8,128)S(1)} %scatter_custom_fusion.8, s32[6144]{0:T(1024)S(1)} %get-tuple-element.176), kind=kCustom, calls=%fused_computation.8.clone | custom fusion | bytes 6316032 | tf_op jit(solution)/shard_map/jvp(jit(_take))/gather | solution.py:102
  386.6 33.4 %scatter_custom_fusion.14 = f32[128,128]{1,0:T(8,128)S(1)} fusion(s32[6144]{0:T(1024)} %param.46, f32[6144,128]{1,0:T(8,128)S(1)} %copy.455, f32[]{:T(128)} %constant.138.clone.1), kind=kCustom, calls=%fused_computation.286 | custom fusion | flops 786432 | bytes 66048 | tf_op jit(solution)/shard_map/jvp()/scatter-add | solution.py:101
  419.9 16.1 %gather_fusion.41 = f32[6144,128]{1,0:T(8,128)S(1)} fusion(f32[128,128]{1,0:T(8,128)S(1)} %scatter_custom_fusion.14, s32[6144]{0:T(1024)S(1)} %get-tuple-element.176), kind=kCustom, calls=%fused_computation.14.clone | custom fusion | bytes 6316032 | tf_op jit(solution)/shard_map/jvp(jit(_take))/gather | solution.py:102
  440.7 33.5 %scatter_custom_fusion.13 = f32[128,128]{1,0:T(8,128)S(1)} fusion(s32[6144]{0:T(1024)} %param.46, f32[6144,128]{1,0:T(8,128)S(1)} %copy.453, f32[]{:T(128)} %constant.138.clone.1), kind=kCustom, calls=%fused_computation.288 | custom fusion | flops 786432 | bytes 66048 | tf_op jit(solution)/shard_map/jvp()/scatter-add | solution.py:101
  474.3 16.1 %gather_fusion.40 = f32[6144,128]{1,0:T(8,128)S(1)} fusion(f32[128,128]{1,0:T(8,128)S(1)} %scatter_custom_fusion.13, s32[6144]{0:T(1024)S(1)} %get-tuple-element.176), kind=kCustom, calls=%fused_computation.13.clone | custom fusion | bytes 6316032 | tf_op jit(solution)/shard_map/jvp(jit(_take))/gather | solution.py:102
  495.1 33.4 %scatter_custom_fusion.12 = f32[128,128]{1,0:T(8,128)S(1)} fusion(s32[6144]{0:T(1024)} %param.46, f32[6144,128]{1,0:T(8,128)S(1)} %copy.451, f32[]{:T(128)} %constant.138.clone.1), kind=kCustom, calls=%fused_computation.290 | custom fusion | flops 786432 | bytes 66048 | tf_op jit(solution)/shard_map/jvp()/scatter-add | solution.py:101
  528.5 16.1 %gather_fusion.39 = f32[6144,128]{1,0:T(8,128)S(1)} fusion(f32[128,128]{1,0:T(8,128)S(1)} %scatter_custom_fusion.12, s32[6144]{0:T(1024)S(1)} %get-tuple-element.176), kind=kCustom, calls=%fused_computation.12.clone | custom fusion | bytes 6316032 | tf_op jit(solution)/shard_map/jvp(jit(_take))/gather | solution.py:102
  549.3 33.4 %scatter_custom_fusion.11 = f32[128,128]{1,0:T(8,128)S(1)} fusion(s32[6144]{0:T(1024)} %param.46, f32[6144,128]{1,0:T(8,128)S(1)} %copy.449, f32[]{:T(128)} %constant.138.clone.1), kind=kCustom, calls=%fused_computation.292 | custom fusion | flops 786432 | bytes 66048 | tf_op jit(solution)/shard_map/jvp()/scatter-add | solution.py:101
  582.7 16.1 %gather_fusion.38 = f32[6144,128]{1,0:T(8,128)S(1)} fusion(f32[128,128]{1,0:T(8,128)S(1)} %scatter_custom_fusion.11, s32[6144]{0:T(1024)S(1)} %get-tuple-element.176), kind=kCustom, calls=%fused_computation.11.clone | custom fusion | bytes 6316032 | tf_op jit(solution)/shard_map/jvp(jit(_take))/gather | solution.py:102
  603.6 33.4 %scatter_custom_fusion.10 = f32[128,128]{1,0:T(8,128)S(1)} fusion(s32[6144]{0:T(1024)} %param.46, f32[6144,128]{1,0:T(8,128)S(1)} %copy.447, f32[]{:T(128)} %constant.138.clone.1), kind=kCustom, calls=%fused_computation.294 | custom fusion | flops 786432 | bytes 66048 | tf_op jit(solution)/shard_map/jvp()/scatter-add | solution.py:101
  636.9 16.1 %gather_fusion.37 = f32[6144,128]{1,0:T(8,128)S(1)} fusion(f32[128,128]{1,0:T(8,128)S(1)} %scatter_custom_fusion.10, s32[6144]{0:T(1024)S(1)} %get-tuple-element.176), kind=kCustom, calls=%fused_computation.10.clone | custom fusion | bytes 6316032 | tf_op jit(solution)/shard_map/jvp(jit(_take))/gather | solution.py:102
  657.8 33.6 %scatter_custom_fusion.9 = f32[128,128]{1,0:T(8,128)S(1)} fusion(s32[6144]{0:T(1024)} %param.46, f32[6144,128]{1,0:T(8,128)S(1)} %copy.445, f32[]{:T(128)} %constant.138.clone.1), kind=kCustom, calls=%fused_computation.296 | custom fusion | flops 786432 | bytes 66048 | tf_op jit(solution)/shard_map/jvp()/scatter-add | solution.py:101
  691.4 20.9 %gather_fusion.36 = f32[6144,128]{1,0:T(8,128)} fusion(f32[128,128]{1,0:T(8,128)S(1)} %scatter_custom_fusion.9, s32[6144]{0:T(1024)S(1)} %get-tuple-element.176), kind=kCustom, calls=%fused_computation.9.clone | custom fusion | bytes 6316032 | tf_op jit(solution)/shard_map/jvp(jit(_take))/gather | solution.py:102
  716.1 13.9 multiply_convert_fusion.1
  737.9 17.9 %broadcast_multiply_fusion.4 = (f32[6144,128]{0,1:T(8,128)}, f32[6144,128]{0,1:T(8,128)}, f32[6144,128]{0,1:T(8,128)}, f32[6144,128]{0,1:T(8,128)}, f32[6144,128...) fusion(f32[6144,128]{0,1:T(8,128)} %get-tuple-element.95, ...), kind=kLoop, calls=%fused_computation.152 | loop fusion | flops 24330240 | bytes 50706432 | tf_op jit(solution)/shard_map/transpose(jvp())/mul | solution.py:102
  769.2 33.9 %scatter_custom_fusion.17 = f32[128,128]{1,0:T(8,128)S(1)} fusion(s32[6144]{0:T(1024)} %get-tuple-element.178, f32[6144,128]{1,0:T(8,128)} %copy.463, f32[]{:T(128)} %constant.138.clone.1), kind=kCustom, calls=%fused_computation.280 | custom fusion | flops 786432 | bytes 66048 | tf_op jit(solution)/shard_map/transpose(jvp(jit(_take)))/scatter-add | solution.py:102
  803.1 16.1 %gather_fusion.15 = f32[6144,128]{1,0:T(8,128)S(1)} fusion(f32[128,128]{1,0:T(8,128)S(1)} %scatter_custom_fusion.17, s32[6144]{0:T(1024)S(1)} %copy-done.17), kind=kCustom, calls=%fused_computation.31 | custom fusion | bytes 6316032 | tf_op jit(solution)/shard_map/transpose(jvp())/gather | solution.py:101
  821.5 33.5 %scatter_custom_fusion.16 = f32[128,128]{1,0:T(8,128)S(1)} fusion(s32[6144]{0:T(1024)} %get-tuple-element.178, f32[6144,128]{1,0:T(8,128)} %copy.461, f32[]{:T(128)} %constant.138.clone.1), kind=kCustom, calls=%fused_computation.282 | custom fusion | flops 786432 | bytes 66048 | tf_op jit(solution)/shard_map/transpose(jvp(jit(_take)))/scatter-add | solution.py:102
  855.0 16.1 %gather_fusion.14 = f32[6144,128]{1,0:T(8,128)S(1)} fusion(f32[128,128]{1,0:T(8,128)S(1)} %scatter_custom_fusion.16, s32[6144]{0:T(1024)S(1)} %copy-done.17), kind=kCustom, calls=%fused_computation.30 | custom fusion | bytes 6316032 | tf_op jit(solution)/shard_map/transpose(jvp())/gather | solution.py:101
  875.9 33.4 %scatter_custom_fusion.21 = f32[128,128]{1,0:T(8,128)S(1)} fusion(s32[6144]{0:T(1024)} %get-tuple-element.178, f32[6144,128]{1,0:T(8,128)S(1)} %copy.471, f32[]{:T(128)} %constant.138.clone.1), kind=kCustom, calls=%fused_computation.272 | custom fusion | flops 786432 | bytes 66048 | tf_op jit(solution)/shard_map/transpose(jvp(jit(_take)))/scatter-add | solution.py:102
  909.2 16.1 %gather_fusion.19 = f32[6144,128]{1,0:T(8,128)S(1)} fusion(f32[128,128]{1,0:T(8,128)S(1)} %scatter_custom_fusion.21, s32[6144]{0:T(1024)S(1)} %copy-done.17), kind=kCustom, calls=%fused_computation.35 | custom fusion | bytes 6316032 | tf_op jit(solution)/shard_map/transpose(jvp())/gather | solution.py:101
  930.0 33.4 %scatter_custom_fusion.18 = f32[128,128]{1,0:T(8,128)S(1)} fusion(s32[6144]{0:T(1024)} %get-tuple-element.178, f32[6144,128]{1,0:T(8,128)S(1)} %copy.465, f32[]{:T(128)} %constant.138.clone.1), kind=kCustom, calls=%fused_computation.278 | custom fusion | flops 786432 | bytes 66048 | tf_op jit(solution)/shard_map/transpose(jvp(jit(_take)))/scatter-add | solution.py:102
  963.4 16.3 %gather_fusion.16 = f32[6144,128]{1,0:T(8,128)S(1)} fusion(f32[128,128]{1,0:T(8,128)S(1)} %scatter_custom_fusion.18, s32[6144]{0:T(1024)S(1)} %copy-done.17), kind=kCustom, calls=%fused_computation.32 | custom fusion | bytes 6316032 | tf_op jit(solution)/shard_map/transpose(jvp())/gather | solution.py:101
  984.4 33.4 %scatter_custom_fusion.22 = f32[128,128]{1,0:T(8,128)S(1)} fusion(s32[6144]{0:T(1024)} %get-tuple-element.178, f32[6144,128]{1,0:T(8,128)S(1)} %copy.473, f32[]{:T(128)} %constant.138.clone.1), kind=kCustom, calls=%fused_computation.270 | custom fusion | flops 786432 | bytes 66048 | tf_op jit(solution)/shard_map/transpose(jvp(jit(_take)))/scatter-add | solution.py:102
  1017.8 16.1 %gather_fusion.20 = f32[6144,128]{1,0:T(8,128)S(1)} fusion(f32[128,128]{1,0:T(8,128)S(1)} %scatter_custom_fusion.22, s32[6144]{0:T(1024)S(1)} %copy-done.17), kind=kCustom, calls=%fused_computation.36 | custom fusion | bytes 6316032 | tf_op jit(solution)/shard_map/transpose(jvp())/gather | solution.py:101
  1038.7 33.4 %scatter_custom_fusion.20 = f32[128,128]{1,0:T(8,128)S(1)} fusion(s32[6144]{0:T(1024)} %get-tuple-element.178, f32[6144,128]{1,0:T(8,128)S(1)} %copy.469, f32[]{:T(128)} %constant.138.clone.1), kind=kCustom, calls=%fused_computation.274 | custom fusion | flops 786432 | bytes 66048 | tf_op jit(solution)/shard_map/transpose(jvp(jit(_take)))/scatter-add | solution.py:102
  1072.1 16.1 %gather_fusion.18 = f32[6144,128]{1,0:T(8,128)S(1)} fusion(f32[128,128]{1,0:T(8,128)S(1)} %scatter_custom_fusion.20, s32[6144]{0:T(1024)S(1)} %copy-done.17), kind=kCustom, calls=%fused_computation.34 | custom fusion | bytes 6316032 | tf_op jit(solution)/shard_map/transpose(jvp())/gather | solution.py:101
  1093.0 33.4 %scatter_custom_fusion.19 = f32[128,128]{1,0:T(8,128)S(1)} fusion(s32[6144]{0:T(1024)} %get-tuple-element.178, f32[6144,128]{1,0:T(8,128)S(1)} %copy.467, f32[]{:T(128)} %constant.138.clone.1), kind=kCustom, calls=%fused_computation.276 | custom fusion | flops 786432 | bytes 66048 | tf_op jit(solution)/shard_map/transpose(jvp(jit(_take)))/scatter-add | solution.py:102
  1126.4 16.1 %gather_fusion.17 = f32[6144,128]{1,0:T(8,128)S(1)} fusion(f32[128,128]{1,0:T(8,128)S(1)} %scatter_custom_fusion.19, s32[6144]{0:T(1024)S(1)} %copy-done.17), kind=kCustom, calls=%fused_computation.33 | custom fusion | bytes 6316032 | tf_op jit(solution)/shard_map/transpose(jvp())/gather | solution.py:101
  1147.2 33.4 %scatter_custom_fusion.15 = f32[128,128]{1,0:T(8,128)S(1)} fusion(s32[6144]{0:T(1024)} %get-tuple-element.178, f32[6144,128]{1,0:T(8,128)S(1)} %copy.459, f32[]{:T(128)} %constant.138.clone.1), kind=kCustom, calls=%fused_computation.284 | custom fusion | flops 786432 | bytes 66048 | tf_op jit(solution)/shard_map/transpose(jvp(jit(_take)))/scatter-add | solution.py:102
  1180.6 16.3 %gather_fusion.13 = f32[6144,128]{1,0:T(8,128)S(1)} fusion(f32[128,128]{1,0:T(8,128)S(1)} %scatter_custom_fusion.15, s32[6144]{0:T(1024)S(1)} %copy-done.17), kind=kCustom, calls=%fused_computation.29 | custom fusion | bytes 6316032 | tf_op jit(solution)/shard_map/transpose(jvp())/gather | solution.py:101
  1199.3 33.5 %scatter_custom_fusion.23 = f32[128,128]{1,0:T(8,128)S(1)} fusion(s32[6144]{0:T(1024)} %get-tuple-element.178, f32[6144,128]{1,0:T(8,128)} %copy.476, f32[]{:T(128)} %constant.138.clone.1), kind=kCustom, calls=%fused_computation.268 | custom fusion | flops 786432 | bytes 66048 | tf_op jit(solution)/shard_map/transpose(jvp(jit(_take)))/scatter-add | solution.py:102
  1232.8 21.0 %gather_fusion.21 = f32[6144,128]{1,0:T(8,128)} fusion(f32[128,128]{1,0:T(8,128)S(1)} %scatter_custom_fusion.23, s32[6144]{0:T(1024)S(1)} %copy-done.17), kind=kCustom, calls=%fused_computation.37 | custom fusion | bytes 6316032 | tf_op jit(solution)/shard_map/transpose(jvp())/gather | solution.py:101
  1284.0 33.5 %scatter_custom_fusion.32 = f32[432,128]{1,0:T(8,128)S(1)} fusion(s32[6144]{0:T(1024)} %get-tuple-element.166, bf16[6144,128]{1,0:T(8,128)(2,1)S(1)} %convolution_convert_fusion.1, f32[]{:T(128)} %constant.138.clone.1), kind=kCustom, calls=%fused_computation.93 | custom fusion | flops 1572864 | bytes 1794560 | tf_op jit(solution)/shard_map/transpose(jvp(jit(_take)))/scatter-add | solution.py:89
  1329.2 33.5 %scatter_custom_fusion.25 = f32[3,432]{0,1:T(8,128)S(1)} fusion(s32[6144]{0:T(1024)} %get-tuple-element.166, f32[6144,3]{1,0:T(8,128)} %copy.481, f32[]{:T(128)} %constant.138.clone.1), kind=kCustom, calls=%fused_computation.223 | custom fusion | flops 18432 | bytes 5696 | tf_op jit(solution)/shard_map/transpose(jvp(jit(_take)))/scatter-add | solution.py:78
  1362.7 33.5 %scatter_custom_fusion.24 = f32[3,432]{0,1:T(8,128)S(1)} fusion(s32[6144]{0:T(1024)} %get-tuple-element.179, f32[6144,3]{1,0:T(8,128)} %copy.480, f32[]{:T(128)} %constant.138.clone.1), kind=kCustom, calls=%fused_computation.225 | custom fusion | flops 18432 | bytes 5696 | tf_op jit(solution)/shard_map/transpose(jvp(jit(_take)))/scatter-add | solution.py:78
  1399.3 33.4 %scatter_custom_fusion.31 = f32[128,128]{1,0:T(8,128)S(1)} fusion(s32[6144]{0:T(1024)} %get-tuple-element.178, bf16[6144,128]{1,0:T(8,128)(2,1)S(1)} %convolution_convert_fusion.1, f32[]{:T(128)} %constant.138.clone.1), kind=kCustom, calls=%fused_computation.95 | custom fusion | flops 1572864 | bytes 1638912 | tf_op jit(solution)/shard_map/transpose(jvp(jit(_take)))/scatter-add | solution.py:89
  1446.9 43.6 %scatter_custom_fusion.30 = f32[128]{0:T(128)} fusion(s32[6144]{0:T(1024)} %param.46, f32[6144]{0:T(1024)S(1)} %get-tuple-element.162, f32[]{:T(128)} %constant.138.clone.1), kind=kCustom, calls=%fused_computation.372 | custom fusion | flops 6144 | bytes 1024 | tf_op jit(solution)/shard_map/jvp()/scatter-add | solution.py:109
  (490 shorter events, 310.4 us)
Async XLA Ops:
  0.6 729.4 %copy-start = (bf16[256,128]{1,0:T(8,128)(2,1)S(1)}, bf16[256,128]{1,0:T(8,128)(2,1)}, u32[]{:S(2)}) copy-start(bf16[256,128]{1,0:T(8,128)(2,1)} %param.55) | copy-start | bytes 196612
  0.6 21.2 %copy-start.82 = (s32[8]{0:T(128)S(1)}, s32[8]{0:T(128)}, u32[]{:S(2)}) copy-start(s32[8]{0:T(128)} %constant.299) | copy-start | bytes 100
  11.5 21.9 %collective-permute-start.1 = (f32[1,3,3,3,32]{4,3,2,1,0:T(4,128)S(1)}, f32[1,3,3,3,32]{4,3,2,1,0:T(4,128)S(1)}, u32[]{:S(2)}, u32[]{:S(2)}) collective-permute-start(f32[1,3,3,3,32]{4,3,2,1,0:T(4,128)S(1)} %bitcast.226), channel_id=1, source_target_pairs={{32,0},{64,32},{96,64},{0,96},{33,1},{65,33},{97,65},{1,97},{34,2}... | collective-permute-start | bytes 10376 | tf_op jit(solution)/shard_map/ppermute | solution.py:19
  15.2 18.3 %collective-permute-start = (f32[1,3,3,3,32]{4,3,2,1,0:T(4,128)S(1)}, f32[1,3,3,3,32]{4,3,2,1,0:T(4,128)S(1)}, u32[]{:S(2)}, u32[]{:S(2)}) collective-permute-start(f32[1,3,3,3,32]{4,3,2,1,0:T(4,128)S(1)} %bitcast.225), channel_id=1, source_target_pairs={{0,32},{32,64},{64,96},{96,0},{1,33},{33,65},{65,97},{97,1},{2,34}... | collective-permute-start | bytes 10376 | tf_op jit(solution)/shard_map/ppermute | solution.py:17
  21.8 25.5 %copy-start.96 = (bf16[128]{0:T(256)(128)(2,1)S(1)}, bf16[128]{0:T(256)(128)(2,1)}, u32[]{:S(2)}) copy-start(bf16[128]{0:T(256)(128)(2,1)} %param.56) | copy-start | bytes 772
  23.4 96.0 %collective-permute-start.7 = (f32[1,3,3,32,128]{4,3,2,1,0:T(8,128)}, f32[1,3,3,32,128]{4,3,2,1,0:T(8,128)}, u32[]{:S(2)}, u32[]{:S(2)}) collective-permute-start(f32[1,3,3,32,128]{4,3,2,1,0:T(8,128)} %bitcast.11), channel_id=1, source_target_pairs={{32,0},{64,32},{96,64},{0,96},{33,1},{65,33},{97,65},{1,97},{34,2}... | collective-permute-start | bytes 442376 | tf_op jit(solution)/shard_map/ppermute | solution.py:19
  26.1 93.4 %collective-permute-start.6 = (f32[1,3,3,32,128]{4,3,2,1,0:T(8,128)}, f32[1,3,3,32,128]{4,3,2,1,0:T(8,128)}, u32[]{:S(2)}, u32[]{:S(2)}) collective-permute-start(f32[1,3,3,32,128]{4,3,2,1,0:T(8,128)} %bitcast.9), channel_id=1, source_target_pairs={{0,32},{32,64},{64,96},{96,0},{1,33},{33,65},{65,97},{97,1},{2,34}... | collective-permute-start | bytes 442376 | tf_op jit(solution)/shard_map/ppermute | solution.py:17
  28.5 42.6 %copy-start.41 = (s32[6144]{0:T(1024)}, s32[6144]{0:T(1024)S(1)}, u32[]{:S(2)}) copy-start(s32[6144]{0:T(1024)S(1)} %get-tuple-element.167) | copy-start | bytes 73732
  33.5 4.1 collective-permute-start.2
  36.6 3.3 collective-permute-start.3
  40.6 23.3 %collective-permute-start.4 = (f32[5,5,1,3,32]{4,3,2,1,0:T(4,128)}, f32[5,5,1,3,32]{4,3,2,1,0:T(4,128)}, u32[]{:S(2)}, u32[]{:S(2)}) collective-permute-start(f32[5,5,1,3,32]{4,3,2,1,0:T(4,128)} %get-tuple-element.142), channel_id=1, source_target_pairs={{0,1},{1,2},{2,3},{3,4},{4,5},{5,6},{6,7},{7,0},{8,9},{9,10},{10,1... | collective-permute-start | bytes 28808 | tf_op jit(solution)/shard_map/ppermute | solution.py:17
  41.8 22.1 %collective-permute-start.5 = (f32[5,5,1,3,32]{4,3,2,1,0:T(4,128)}, f32[5,5,1,3,32]{4,3,2,1,0:T(4,128)}, u32[]{:S(2)}, u32[]{:S(2)}) collective-permute-start(f32[5,5,1,3,32]{4,3,2,1,0:T(4,128)} %get-tuple-element.143), channel_id=1, source_target_pairs={{1,0},{2,1},{3,2},{4,3},{5,4},{6,5},{7,6},{0,7},{9,8},{10,9},{11,1... | collective-permute-start | bytes 28808 | tf_op jit(solution)/shard_map/ppermute | solution.py:19
  47.8 21.8 %copy-start.90 = (f32[3,128]{1,0:T(4,128)S(1)}, f32[3,128]{1,0:T(4,128)}, u32[]{:S(2)}) copy-start(f32[3,128]{1,0:T(4,128)} %param.41) | copy-start | bytes 4612
  118.6 24.8 %copy-start.13 = (f32[27,32,128]{2,1,0:T(8,128)S(1)}, f32[27,32,128]{2,1,0:T(8,128)}, u32[]{:S(2)}) copy-start(f32[27,32,128]{2,1,0:T(8,128)} %pad_maximum_fusion.2) | copy-start | bytes 1327108
  118.8 27.2 %copy-start.42 = (f32[6144]{0:T(1024)}, f32[6144]{0:T(1024)S(1)}, u32[]{:S(2)}) copy-start(f32[6144]{0:T(1024)S(1)} %get-tuple-element.100) | copy-start | bytes 73732
  120.6 5.2 collective-permute-start.8
  120.8 6.5 collective-permute-start.9
  121.2 22.2 %copy-start.32 = (f32[3,6144]{1,0:T(4,128)}, f32[3,6144]{1,0:T(4,128)S(1)}, u32[]{:S(2)}) copy-start(f32[3,6144]{1,0:T(4,128)S(1)} %broadcast_divide_fusion) | copy-start | bytes 221188
  128.4 15.0 collective-permute-start.10
  128.5 14.9 collective-permute-start.11
  158.1 23.2 %copy-start.37 = (f32[6144]{0:T(1024)S(1)}, f32[6144]{0:T(1024)}, u32[]{:S(2)}) copy-start(f32[6144]{0:T(1024)} %copy-done.36) | copy-start | bytes 73732
  158.1 23.2 %copy-start.69 = (f32[6144]{0:T(1024)S(1)}, f32[6144]{0:T(1024)}, u32[]{:S(2)}) copy-start(f32[6144]{0:T(1024)} %get-tuple-element.170) | copy-start | bytes 73732
  158.1 23.2 %copy-start.74 = (pred[6144]{0:T(1024)(128)(4,1)S(1)}, pred[6144]{0:T(1024)(128)(4,1)}, u32[]{:S(2)}) copy-start(pred[6144]{0:T(1024)(128)(4,1)} %get-tuple-element.187) | copy-start | bytes 18436
  158.1 23.2 %copy-start.91 = (f32[8,128]{1,0:T(8,128)S(1)}, f32[8,128]{1,0:T(8,128)}, u32[]{:S(2)}) copy-start(f32[8,128]{1,0:T(8,128)} %param.51) | copy-start | bytes 12292
  158.1 23.2 %copy-start.92 = (f32[8]{0:T(128)S(1)}, f32[8]{0:T(128)}, u32[]{:S(2)}) copy-start(f32[8]{0:T(128)} %convert_multiply_fusion.4) | copy-start | bytes 100
  198.5 123.6 %copy-start.2 = (f32[6144,128]{0,1:T(8,128)}, f32[6144,128]{0,1:T(8,128)S(1)}, u32[]{:S(2)}) copy-start(f32[6144,128]{0,1:T(8,128)S(1)} %get-tuple-element.99) | copy-start | bytes 9437188
  766.8 36.2 %copy-start.17 = (s32[6144]{0:T(1024)S(1)}, s32[6144]{0:T(1024)}, u32[]{:S(2)}) copy-start(s32[6144]{0:T(1024)} %get-tuple-element.175) | copy-start | bytes 73732
  1279.1 38.4 %copy-start.22 = (f32[128,128]{1,0:T(8,128)S(1)}, f32[128,128]{1,0:T(8,128)}, u32[]{:S(2)}) copy-start(f32[128,128]{1,0:T(8,128)} %param.50) | copy-start | bytes 196612
  1279.1 38.8 %copy-start.80 = (s32[6]{0:T(128)S(1)}, s32[6]{0:T(128)}, u32[]{:S(2)}) copy-start(s32[6]{0:T(128)} %constant.297) | copy-start | bytes 76
  1284.0 35.1 %copy-start.83 = (s32[8]{0:T(128)S(1)}, s32[8]{0:T(128)}, u32[]{:S(2)}) copy-start(s32[8]{0:T(128)} %constant.299) | copy-start | bytes 100
  1284.0 35.9 %copy-start.86 = (s32[12]{0:T(128)S(1)}, s32[12]{0:T(128)}, u32[]{:S(2)}) copy-start(s32[12]{0:T(128)} %constant.298) | copy-start | bytes 148
  1326.9 69.8 %copy-start.84 = (s32[8]{0:T(128)S(1)}, s32[8]{0:T(128)}, u32[]{:S(2)}) copy-start(s32[8]{0:T(128)} %constant.299) | copy-start | bytes 100
  1326.9 70.6 %copy-start.87 = (s32[12]{0:T(128)S(1)}, s32[12]{0:T(128)}, u32[]{:S(2)}) copy-start(s32[12]{0:T(128)} %constant.298) | copy-start | bytes 148
  1326.9 71.5 %copy-start.81 = (s32[6]{0:T(128)S(1)}, s32[6]{0:T(128)}, u32[]{:S(2)}) copy-start(s32[6]{0:T(128)} %constant.297) | copy-start | bytes 76
  1327.0 105.8 %copy-start.40 = (f32[128,128]{1,0:T(8,128)S(1)}, f32[128,128]{1,0:T(8,128)}, u32[]{:S(2)}) copy-start(f32[128,128]{1,0:T(8,128)} %param.49) | copy-start | bytes 196612
  1329.2 109.7 %copy-start.89 = (f32[27]{0:T(128)S(1)}, f32[27]{0:T(128)}, u32[]{:S(2)}) copy-start(f32[27]{0:T(128)} %copy-done.88) | copy-start | bytes 328
  1433.0 63.5 %collective-permute-start.19 = (f32[1,3,3,32,128]{4,3,2,1,0:T(8,128)S(1)}, f32[1,3,3,32,128]{4,3,2,1,0:T(8,128)S(1)}, u32[]{:S(2)}, u32[]{:S(2)}) collective-permute-start(f32[1,3,3,32,128]{4,3,2,1,0:T(8,128)S(1)} %bitcast.201), channel_id=1, source_target_pairs={{32,0},{64,32},{96,64},{0,96},{33,1},{65,33},{97,65},{1,97},{34,2}... | collective-permute-start | bytes 442376 | tf_op jit(solution)/shard_map/ppermute | solution.py:19
  1436.1 60.5 %collective-permute-start.18 = (f32[1,3,3,32,128]{4,3,2,1,0:T(8,128)S(1)}, f32[1,3,3,32,128]{4,3,2,1,0:T(8,128)S(1)}, u32[]{:S(2)}, u32[]{:S(2)}) collective-permute-start(f32[1,3,3,32,128]{4,3,2,1,0:T(8,128)S(1)} %bitcast.200), channel_id=1, source_target_pairs={{0,32},{32,64},{64,96},{96,0},{1,33},{33,65},{65,97},{97,1},{2,34}... | collective-permute-start | bytes 442376 | tf_op jit(solution)/shard_map/ppermute | solution.py:17
  1436.1 3.7 collective-permute-start.13
  1438.8 4.4 collective-permute-start.12
  1443.2 47.2 %collective-permute-start.14 = (f32[5,1,3,3,32]{4,3,2,1,0:T(4,128)S(1)}, f32[5,1,3,3,32]{4,3,2,1,0:T(4,128)S(1)}, u32[]{:S(2)}, u32[]{:S(2)}) collective-permute-start(f32[5,1,3,3,32]{4,3,2,1,0:T(4,128)S(1)} %get-tuple-element.150), channel_id=1, source_target_pairs={{0,8},{8,16},{16,24},{24,0},{1,9},{9,17},{17,25},{25,1},{2,10},{10... | collective-permute-start | bytes 17288 | tf_op jit(solution)/shard_map/ppermute | solution.py:17
  1446.6 43.9 %collective-permute-start.15 = (f32[5,1,3,3,32]{4,3,2,1,0:T(4,128)S(1)}, f32[5,1,3,3,32]{4,3,2,1,0:T(4,128)S(1)}, u32[]{:S(2)}, u32[]{:S(2)}) collective-permute-start(f32[5,1,3,3,32]{4,3,2,1,0:T(4,128)S(1)} %get-tuple-element.151), channel_id=1, source_target_pairs={{8,0},{16,8},{24,16},{0,24},{9,1},{17,9},{25,17},{1,25},{10,2},{18... | collective-permute-start | bytes 17288 | tf_op jit(solution)/shard_map/ppermute | solution.py:19
  1490.5 8.1 collective-permute-start.16
  1490.5 8.1 collective-permute-start.17
  1496.6 6.5 collective-permute-start.20
  1498.1 6.4 collective-permute-start.21
  1504.6 15.0 collective-permute-start.22
  1504.7 15.7 %collective-permute-start.23 = (f32[5,5,1,32,128]{4,3,2,1,0:T(8,128)S(1)}, f32[5,5,1,32,128]{4,3,2,1,0:T(8,128)}, u32[]{:S(2)}, u32[]{:S(2)}) collective-permute-start(f32[5,5,1,32,128]{4,3,2,1,0:T(8,128)S(1)} %get-tuple-element.125), channel_id=1, source_target_pairs={{1,0},{2,1},{3,2},{4,3},{5,4},{6,5},{7,6},{0,7},{9,8},{10,9},{11,1... | collective-permute-start | bytes 1228808 | tf_op jit(solution)/shard_map/ppermute | solution.py:19
  (75 other events, 458.6 us)
where the time goes:
time: 1540 us; the launch traced here: 1530 us
  other arithmetic  856 us (56%)
  local copies, waits for them, and re-layouts  545 us (35%)
  matrix products  48.4 us (3%)
  starting transfers between devices  42.7 us (3%)
  waiting for transfers between devices  31.6 us (2%)
    scatter-add x9, other arithmetic, local_energy(): jax.ops.segment_sum(env_weight * comp[:, None], centre, num_segments=n_own)  302 us
    scatter-add x9, other arithmetic, local_energy(): total = total + comp[:, None] * jnp.take(env_m, centre, axis=0)  301 us
    gather x18, local copies, waits for them, and re-layouts, local_energy(): total = total + comp[:, None] * jnp.take(env_m, centre, axis=0)  184 us
    gather x18, local copies, waits for them, and re-layouts, local_energy(): jax.ops.segment_sum(env_weight * comp[:, None], centre, num_segments=n_own)  173 us
    scatter-add x2, other arithmetic, local_energy(): disp = jnp.take(pos_tab, other, axis=1) - jnp.take(pos_tab, centre, axis=1)  67 us
    gather x4, local copies, waits for them, and re-layouts, local_energy(): disp = jnp.take(pos_tab, other, axis=1) - jnp.take(pos_tab, centre, axis=1)  47.5 us
    scatter-add x1, other arithmetic, local_energy(): atom_energy = jax.ops.segment_sum(edge_energy, centre, num_segments=n_own)  43.6 us
    scatter-add x1, other arithmetic, local_energy(): jnp.take(proj_b, other, axis=0)  33.5 us
  transfers between devices with their start and end apart: 24, of which 11 were waited for; matrix products, arithmetic and copies ran while one was open for 9% of the time, Pallas kernels for 0%

commit v1 on v0

v1 whole, which is shorter than its diff:
```python
import functools
import math
import jax
import jax.numpy as jnp
import numpy as np
from jax import lax
from jax.experimental import pallas as pl
from jax.experimental.pallas import tpu as pltpu
from jax.sharding import PartitionSpec as P

F32, BF16 = jnp.float32, jnp.bfloat16
NT = (((1,), (1,)), ((), ()))
NN = (((1,), (0,)), ((), ()))
TN = (((0,), (0,)), ((), ()))
TT = (((0,), (1,)), ((), ()))
ROWS = 608

def dot(a, b, dims=NN):
    return lax.dot_general(a, b, dims, preferred_element_type=F32)

def split(x, n):
    parts = []
    for _ in range(n):
        p = x.astype(BF16)
        parts.append(p)
        x = x - p.astype(F32)
    return parts

def sincos_turns(t):
    f = t - jnp.round(t)
    f2 = f * f
    s = f * _poly(f2, _SC)
    c = _poly(f2, _CC)
    return s, c

def _fit(fun, deg):
    x = np.cos(np.pi * (np.arange(400) + 0.5) / 400) * 0.125 + 0.125
    ch = np.polynomial.chebyshev.Chebyshev.fit(x, fun(x), deg, domain=[0, 0.25])
    return [float(v) for v in ch.convert(kind=np.polynomial.Polynomial).coef]

_SC = _fit(lambda y: np.sin(2 * np.pi * np.sqrt(y)) / np.sqrt(y), 7)
_CC = _fit(lambda y: np.cos(2 * np.pi * np.sqrt(y)), 7)

def _poly(x, cs):
    acc = cs[-1]
    for c in cs[-2::-1]:
        acc = acc * x + c
    return acc

def onehots(c, o, iota):
    cb = c.astype(F32).astype(BF16)
    far = jnp.maximum(o - 416, 0)
    o = jnp.where(o < 416, o, 416 + (far >> 1) * 8 + (far & 1))
    mask_c = iota == cb
    one, zero = jnp.ones((), BF16), jnp.zeros((), BF16)
    tiles = [jnp.where(mask_c, one, zero)]
    for t in range(4):
        ob = (o - 128 * t).astype(F32).astype(BF16)
        n = 128 if t < 3 else 96
        tiles.append(jnp.where(iota[:n] == ob, one, zero))
    return jnp.concatenate(tiles, axis=0)

def harm(ux, uy, uz):
    return [1.732 * ux * uy, 1.732 * uy * uz, 1.732 * ux * uz,
            0.866 * (ux * ux - uy * uy), 0.5 * (3.0 * uz * uz - 1.0)]

def weighted(mask, rows):
    zero = jnp.zeros((), BF16)
    return jnp.concatenate([jnp.where(mask, r.astype(BF16), zero) for r in rows], axis=0)

def assemble(env, scale):
    e = [env[:, 128 * m:128 * (m + 1)] * scale for m in range(9)]
    k = 1.732
    top = jnp.concatenate([e[0] - 0.5 * e[8], 0.5 * e[1], 0.5 * e[2], 0.5 * e[3]], axis=1)
    rx = jnp.concatenate([e[1], k * e[7], k * e[4], k * e[6]], axis=1)
    ry = jnp.concatenate([e[2], k * e[4], -k * e[7], k * e[5]], axis=1)
    rz = jnp.concatenate([e[3], k * e[6], k * e[5], 3.0 * e[8]], axis=1)
    return jnp.concatenate([top, rx, ry, rz], axis=0).astype(BF16)

def edge_kernel(eb, count_ref, centre_ref, other_ref, pos_ref, feat_ref, ghost_ref, pb_ref,
                wpa_ref, wr_ref, w1_ref, we_ref, wv_ref, w2_ref, wout_ref,
                grad_ref,
                first_s, slope_s, q_s, v_s, ds2_s, dv_s, rows_s, bp_s, tab_s, env_s, left_s, acc_s):
    E = centre_ref.shape[1]
    n = E // eb
    high = lax.Precision.HIGHEST
    iota = lax.broadcasted_iota(jnp.int32, (128, eb), 0).astype(F32).astype(BF16)
    pa = jnp.dot(feat_ref[...], wpa_ref[...], precision=high, preferred_element_type=F32)
    pos = pos_ref[...]
    own = pos
    ghost = ghost_ref[...]
    gpos = jnp.concatenate([ghost[:, 128:], jnp.zeros((32, 128), F32)], axis=0).T[:8, :352]
    top = jnp.concatenate([pa.T, pb_ref[...].T, jnp.concatenate([ghost[:, :128], jnp.zeros((32, 128), F32)], axis=0).T[:, :352]], axis=1)
    tab_s[0:128, :] = top.astype(BF16)
    low = jnp.concatenate([-own, own, gpos], axis=1)
    parts = split(low, 3)
    tab_s[128:160, :] = jnp.concatenate([p.astype(F32) for p in parts] + [jnp.zeros_like(low)], axis=0).astype(BF16)
    w1 = w1_ref[...]
    w1t = w1.astype(F32).T.astype(BF16)
    wevt = jnp.concatenate([we_ref[...].astype(F32).T, wv_ref[...].astype(F32).T], axis=0).astype(BF16)
    w2 = w2_ref[...]
    w2t = w2.astype(F32).T.astype(BF16)
    wback = jnp.concatenate([w2[:128], wv_ref[...], we_ref[...]], axis=1)
    w2b = w2[128:]
    wr = wr_ref[...]
    wr_hi = wr.astype(BF16).astype(F32)
    wr_lo = wr - wr_hi
    wrt = jnp.concatenate([wr_hi, wr_lo, wr_hi, jnp.zeros_like(wr)], axis=0).T.astype(BF16)
    wr2 = jnp.concatenate([wr_hi, wr_lo], axis=0).astype(BF16)
    wout = jnp.broadcast_to(wout_ref[...].astype(F32), (128, 128))
    wout = jnp.concatenate([wout] * (eb // 128), axis=1)
    count = count_ref[0]

    env_s[...] = jnp.zeros_like(env_s)

    def pass_a(i, _):
        ds = pl.ds(pl.multiple_of(i * eb, eb), eb)
        c, o = centre_ref[:, ds], other_ref[:, ds]
        oh = onehots(c, o, iota)
        p = dot(tab_s[...], oh)
        disp = p[128:136] + p[136:144] + p[144:152]
        dx, dy, dz = disp[0:1], disp[1:2], disp[2:3]
        sq = dx * dx + dy * dy + dz * dz + 0.01
        inv = lax.rsqrt(sq)
        dist = sq * inv
        ux, uy, uz = dx * inv, dy * inv, dz * inv
        s4 = 1.0 + 0.25 * dist * dist
        is4 = 1.0 / s4
        g = is4 * is4
        gd = -dist * g * is4
        lane = lax.broadcasted_iota(jnp.int32, (1, eb), 1) + i * eb
        valid = jnp.where(lane < count, 1.0, 0.0)
        gv = g * valid
        h = g * inv
        hd = (gd - h) * inv
        order = lax.broadcasted_iota(jnp.int32, (8, eb), 0).astype(F32) + 1.0
        sn, cs = sincos_turns(order * (0.25 * dist))
        basis = sn * h
        bp_s[:, ds] = order * (math.pi / 2) * cs * h + sn * hd
        rows_s[0:8, ds] = jnp.concatenate([ux, uy, uz, gv, inv, valid, gd, jnp.zeros_like(gd)], axis=0)
        b_hi = basis.astype(BF16).astype(F32)
        b4 = jnp.concatenate([b_hi, b_hi, basis - b_hi, jnp.zeros_like(basis)], axis=0).astype(BF16)
        mixed = (p[:128] + dot(wrt, b4)).astype(BF16)
        z1 = dot(w1t, mixed)
        sg = 0.5 * jnp.tanh(0.5 * z1) + 0.5
        f = z1 * sg
        first = f.astype(BF16)
        first_s[:, ds] = first
        slope_s[:, ds] = ((sg + f * (1.0 - sg)) * gv).astype(BF16)
        qv = dot(wevt, first).astype(BF16)
        q_s[:, ds] = qv[:128]
        v_s[:, ds] = qv[128:]
        g9 = weighted(iota == c.astype(F32).astype(BF16),
                      [gv, gv * ux, gv * uy, gv * uz] + [gv * y for y in harm(ux, uy, uz)])
        env_s[...] += dot(qv[:128], g9, NT)
        return 0
    lax.fori_loop(0, n, pass_a, 0)

    left_s[...] = assemble(env_s[...], 0.2)
    env_s[...] = jnp.zeros_like(env_s)

    def pass_b(i, _):
        ds = pl.ds(pl.multiple_of(i * eb, eb), eb)
        c = centre_ref[:, ds]
        rows = rows_s[:, ds]
        ux, uy, uz, gv = rows[0:1], rows[1:2], rows[2:3], rows[3:4]
        mask = iota == c.astype(F32).astype(BF16)
        m4 = weighted(mask, [jnp.ones_like(ux), ux, uy, uz])
        t4 = dot(left_s[...], m4)
        tx, ty, tz = t4[128:256], t4[256:384], t4[384:512]
        t = t4[:128] + (0.5 * ux) * tx + (0.5 * uy) * ty + (0.5 * uz) * tz
        v = v_s[:, ds].astype(F32)
        scal = (v * t).astype(BF16)
        z2 = dot(w2t, jnp.concatenate([first_s[:, ds], scal], axis=0))
        sg = 0.5 * jnp.tanh(0.5 * z2) + 0.5
        f = z2 * sg
        eo = jnp.sum(f.astype(BF16).astype(F32) * wout, axis=0, keepdims=True)
        ds2 = (wout * (sg + f * (1.0 - sg))).astype(BF16)
        ds2_s[:, ds] = ds2
        dsc = dot(w2b, ds2)
        dv_s[:, ds] = (t * dsc).astype(BF16)
        y = v * dsc
        du = [jnp.sum(y * k, axis=0, keepdims=True) for k in (tx, ty, tz)]
        rows_s[8:16, ds] = jnp.concatenate(du + [eo] + [jnp.zeros((4, eb), F32)], axis=0)
        g9 = jnp.concatenate([m4, weighted(mask, harm(ux, uy, uz))], axis=0)
        env_s[...] += dot((y * gv).astype(BF16), g9, NT)
        return 0
    lax.fori_loop(0, n, pass_b, 0)

    left_s[...] = assemble(env_s[...], 0.2)
    acc_s[...] = jnp.zeros_like(acc_s)

    def pass_c(i, _):
        ds = pl.ds(pl.multiple_of(i * eb, eb), eb)
        c, o = centre_ref[:, ds], other_ref[:, ds]
        rows = rows_s[:, ds]
        ux, uy, uz, gv = rows[0:1], rows[1:2], rows[2:3], rows[3:4]
        inv, valid, gd = rows[4:5], rows[5:6], rows[6:7]
        oh = onehots(c, o, iota)
        mask = iota == c.astype(F32).astype(BF16)
        m4 = weighted(mask, [jnp.ones_like(ux), ux, uy, uz])
        d4 = dot(left_s[...], m4)
        kx, ky, kz = d4[128:256], d4[256:384], d4[384:512]
        d = d4[:128] + (0.5 * ux) * kx + (0.5 * uy) * ky + (0.5 * uz) * kz
        q = q_s[:, ds].astype(F32)
        du = [jnp.sum(q * k, axis=0, keepdims=True) for k in (kx, ky, kz)]
        dgq = jnp.sum(q * d, axis=0, keepdims=True)
        df = dot(wback, jnp.concatenate([ds2_s[:, ds], dv_s[:, ds], d.astype(BF16)], axis=0))
        dz = (df * slope_s[:, ds].astype(F32)).astype(BF16)
        dm = dot(w1, dz).astype(BF16)
        db = dot(wr2, dm)
        db = db[:8] + db[8:]
        eo = rows[11:12]
        dux, duy, duz = [gv * (du[k] + rows[8 + k:9 + k]) for k in range(3)]
        dd = jnp.sum(db * bp_s[:, ds], axis=0, keepdims=True) + valid * (eo + dgq) * gd
        dd = dd - (dux * ux + duy * uy + duz * uz) * inv
        ee = eo * gv
        tail = jnp.concatenate([dux * inv + dd * ux, duy * inv + dd * uy, duz * inv + dd * uz, ee,
                                jnp.zeros((4, eb), F32)], axis=0)
        t_hi = tail.astype(BF16).astype(F32)
        low = jnp.concatenate([t_hi, tail - t_hi], axis=0).astype(BF16)
        acc_s[...] += dot(oh, jnp.concatenate([dm, low], axis=0), NT)
        return 0
    lax.fori_loop(0, n, pass_c, 0)
    acc = acc_s[...]
    low = acc[:, 128:136] + acc[:, 136:144]
    grad_ref[:, 0:128] = acc[:, :128]
    grad_ref[:, 128:256] = jnp.concatenate([low, jnp.zeros((ROWS, 120), F32)], axis=1)

def edge_call(count, centre, other, pos, feat, ghost, pb, wpa, wr, w1, we, wv, w2, wout, eb=3072):
    E = centre.shape[1]
    vm = pl.BlockSpec(memory_space=pltpu.VMEM)
    return pl.pallas_call(
        functools.partial(edge_kernel, eb),
        out_shape=jax.ShapeDtypeStruct((ROWS, 256), F32),
        in_specs=[pl.BlockSpec(memory_space=pltpu.SMEM)] + [vm] * 13,
        out_specs=vm,
        scratch_shapes=[pltpu.VMEM((128, E), BF16)] * 6 + [
            pltpu.VMEM((16, E), F32), pltpu.VMEM((8, E), F32),
            pltpu.VMEM((160, ROWS), BF16), pltpu.VMEM((128, 1152), F32), pltpu.VMEM((512, 512), BF16),
            pltpu.VMEM((ROWS, 144), F32)],
        compiler_params=pltpu.CompilerParams(vmem_limit_bytes=56 * 2**20),
    )(count, centre, other, pos, feat, ghost, pb, wpa, wr, w1, we, wv, w2, wout)


MESH = pl.DeviceIdType.MESH
GHOSTS = 352


def offset_list():
    cells = [(a, b, c) for a in (-1, 0, 1) for b in (-1, 0, 1) for c in (-1, 0, 1) if a or b or c]
    return sorted(cells, key=lambda o: abs(o[0]) + abs(o[1]) + abs(o[2]))


def blocks():
    out, start = [], 0
    for o in offset_list():
        width = (32, 8, 8)[abs(o[0]) + abs(o[1]) + abs(o[2]) - 1]
        out.append((o, start, width))
        start += width
    return out


def partner(offset, sign, sizes):
    at = [lax.axis_index(a) for a in ("gx", "gy", "gz")]
    return tuple(lax.rem(i + sign * o + n, n) for i, o, n in zip(at, offset, sizes))


def greet(sizes):
    barrier = pltpu.get_barrier_semaphore()
    for o in offset_list():
        pl.semaphore_signal(barrier, inc=1, device_id=partner(o, 1, sizes), device_id_type=MESH)
    pl.semaphore_wait(barrier, 26)


def exchange(src, base, dst, send, recv, sign, sizes):
    copies = []
    for k, (o, start, width) in enumerate(blocks()):
        copies.append(
            pltpu.make_async_remote_copy(
                src_ref=src.at[pl.ds(base + start, width)],
                dst_ref=dst.at[pl.ds(start, width)],
                send_sem=send.at[k],
                recv_sem=recv.at[k],
                device_id=partner(o, sign, sizes),
                device_id_type=MESH,
            )
        )
    for copy in copies:
        copy.start()
    return copies


def ghost_kernel(sizes, idx_ref, pos_ref, feat_ref, wpb_ref, ghost_ref, pb_ref, pos8_ref, out_s, in_s, send, recv):
    barrier = pltpu.get_barrier_semaphore()
    for o in offset_list():
        pl.semaphore_signal(barrier, inc=1, device_id=partner(o, 1, sizes), device_id_type=MESH)
    pb = jnp.dot(feat_ref[...], wpb_ref[...], precision=lax.Precision.HIGHEST, preferred_element_type=F32)
    pb_ref[...] = pb
    pos = jnp.concatenate([pos_ref[...], jnp.zeros((5, 128), F32)], axis=0)
    pos8_ref[...] = pos
    pick = (lax.broadcasted_iota(jnp.int32, (128, GHOSTS), 0) == idx_ref[...]).astype(F32).astype(BF16)
    out_s[:, 0:128] = dot(pick, pb.astype(BF16), TN)
    parts = jnp.concatenate([p.astype(F32) for p in split(pos, 3)], axis=0).astype(BF16)
    low = dot(parts, pick)
    low = low[0:8] + low[8:16] + low[16:24]
    low = jnp.concatenate([low, jnp.zeros((120, GHOSTS), F32)], axis=0)
    low = jnp.concatenate([low, jnp.zeros((128, 384 - GHOSTS), F32)], axis=1)
    out_s[:, 128:256] = low.T[:GHOSTS]
    pl.semaphore_wait(barrier, 26)
    copies = exchange(out_s, 0, in_s, send, recv, 1, sizes)
    for copy in copies:
        copy.wait()
    ghost_ref[...] = in_s[...]


def return_kernel(sizes, grad_ref, idx_ref, wpa_ref, wpb_ref, force_ref, energy_ref, fgrad_ref, in_s, send, recv):
    high = lax.Precision.HIGHEST
    greet(sizes)
    copies = exchange(grad_ref, 256, in_s, send, recv, -1, sizes)
    pick = (lax.broadcasted_iota(jnp.int32, (128, GHOSTS), 0) == idx_ref[...]).astype(F32)
    for copy in copies:
        copy.wait()
    own = grad_ref[128:256, :] + jnp.dot(pick, in_s[...], precision=high, preferred_element_type=F32)
    mid = grad_ref[0:128, :]
    fgrad_ref[...] = lax.dot_general(mid[:, :128], wpa_ref[...], NT, precision=high, preferred_element_type=F32) + lax.dot_general(
        own[:, :128], wpb_ref[...], NT, precision=high, preferred_element_type=F32
    )
    mid_t, own_t = mid[:, 128:].T, own[:, 128:].T
    force_ref[...] = mid_t[0:3] - own_t[0:3]
    energy_ref[...] = mid_t[3:4]


def local(
    sizes,
    positions,
    atom_features,
    send_face,
    send_edge,
    send_corner,
    centre,
    other,
    edge_count,
    w_proj_a,
    w_proj_b,
    w_radial,
    w_first,
    w_env,
    w_value,
    w_second,
    w_out,
):
    vm = pl.BlockSpec(memory_space=pltpu.VMEM)
    sems = [pltpu.SemaphoreType.DMA((26,)), pltpu.SemaphoreType.DMA((26,))]
    corner = jnp.pad(send_corner[0], ((0, 0), (0, 6)), constant_values=-1)
    idx = jnp.concatenate([send_face[0].reshape(-1), send_edge[0].reshape(-1), corner.reshape(-1)]).reshape(1, GHOSTS)
    ghost, pb, pos8 = pl.pallas_call(
        functools.partial(ghost_kernel, sizes),
        out_shape=[
            jax.ShapeDtypeStruct((GHOSTS, 256), F32),
            jax.ShapeDtypeStruct((128, 128), F32),
            jax.ShapeDtypeStruct((8, 128), F32),
        ],
        in_specs=[vm] * 4,
        out_specs=[vm] * 3,
        scratch_shapes=[pltpu.VMEM((GHOSTS, 256), F32), pltpu.VMEM((GHOSTS, 256), F32)] + sems,
        compiler_params=pltpu.CompilerParams(collective_id=0, has_side_effects=True),
    )(idx, positions, atom_features, w_proj_b)
    grad = edge_call(
        edge_count,
        centre.reshape(1, -1),
        other.reshape(1, -1),
        pos8,
        atom_features,
        ghost,
        pb,
        w_proj_a,
        w_radial,
        w_first,
        w_env,
        w_value,
        w_second,
        w_out.reshape(-1, 1),
    )
    force, energy, fgrad = pl.pallas_call(
        functools.partial(return_kernel, sizes),
        out_shape=[
            jax.ShapeDtypeStruct((3, 128), F32),
            jax.ShapeDtypeStruct((1, 128), F32),
            jax.ShapeDtypeStruct((128, 128), F32),
        ],
        in_specs=[vm] * 4,
        out_specs=[vm] * 3,
        scratch_shapes=[pltpu.VMEM((GHOSTS, 256), F32)] + sems,
        compiler_params=pltpu.CompilerParams(collective_id=1, has_side_effects=True),
    )(grad, idx, w_proj_a, w_proj_b)
    return force, energy.reshape(-1), fgrad


def solution(mesh):
    sizes = tuple(mesh.shape[a] for a in ("gx", "gy", "gz"))
    axes = ("gx", "gy", "gz")
    return jax.shard_map(
        functools.partial(local, sizes),
        mesh=mesh,
        in_specs=(
            P(None, axes),
            P(axes, None),
            P(axes, None, None),
            P(axes, None, None),
            P(axes, None, None),
            P(axes),
            P(axes),
            P(axes),
        )
        + (P(),) * 8,
        out_specs=(P(None, axes), P(axes), P(axes, None)),
        check_vma=False,
    )
```

time: 1540 us -> 69.3 us (0.04)
  other arithmetic: 856 us -> 0.09 us
  local copies, waits for them, and re-layouts: 545 us -> 6.92 us
  Pallas kernels: 0 us -> 60.6 us
  matrix products: 48.4 us -> 0 us
  starting transfers between devices: 42.7 us -> 0 us
  waiting for transfers between devices: 31.6 us -> 0 us
    scatter-add x25 -> x0, other arithmetic: 784 us -> none  [the longest x9 302 us: local_energy(): jax.ops.segment_sum(env_weight * comp[:, None], centre, num_segments=n_own)]
    gather x67 -> x0, local copies, waits for them, and re-layouts: 469 us -> none  [the longest x18 184 us: local_energy(): total = total + comp[:, None] * jnp.take(env_m, centre, axis=0)]
    pallas_call x0 -> x3, Pallas kernels: none -> 60.6 us  [the longest x1 30.3 us: edge_call(): pl.pallas_call(functools.partial(edge_kernel, eb), out_shape=jax.ShapeDty...]
    dot_general x16 -> x0, matrix products: 48.4 us -> none  [the longest x2 17.5 us: local_energy(): value = jnp.dot(first, w_value, preferred_element_type=jnp.float32)]
    mul x18 -> x0, local copies, waits for them, and re-layouts: 47.5 us -> none  [the longest x8 21.2 us: local_energy(): env_weight * comp[:, None]]
    ppermute x24 -> x0, starting transfers between devices: 42.7 us -> none  [the longest x12 33.1 us: padded(): lax.ppermute(head, axis, [((i + 1) % count, i) for i in range(count)])]
    ppermute x24 -> x0, waiting for transfers between devices: 31.6 us -> none  [the longest x12 25.6 us: padded(): lax.ppermute(tail, axis, [(i, (i + 1) % count) for i in range(count)])]
    mul x8 -> x0, other arithmetic: 30.5 us -> none  [the longest x2 21.5 us: local_energy(): total = total + comp[:, None] * jnp.take(env_m, centre, axis=0)]
  transfers between devices with their start and end apart: 24 -> 0, of which waited for: 11 -> 0; matrix products, arithmetic and copies ran while one was open for 9% -> 0% of each run, Pallas kernels for 0% -> 0%
where the time goes in v1:
time: 69.3 us; the launch traced here: 68.9 us
  Pallas kernels  60.6 us (87%)
  local copies, waits for them, and re-layouts  6.92 us (10%)
  between operations  1.33 us (2%)
    pallas_call x1, Pallas kernels, edge_call(): pl.pallas_call(functools.partial(edge_kernel, eb), out_shape=jax.ShapeDty...  30.3 us
    pallas_call x1, Pallas kernels, local(): pl.pallas_call(functools.partial(ghost_kernel, sizes), out_shape=[jax.Sha...  16.7 us
    pallas_call x1, Pallas kernels, local(): pl.pallas_call(functools.partial(return_kernel, sizes), out_shape=[jax.Sh...  13.6 us
    unnamed x17, local copies, waits for them, and re-layouts  5.37 us

profile of v1, /device:TPU:1, one launch (start us, length us, event | category | flops | bytes accessed | tf_op | source)
XLA Modules:
  0.0 68.9 jit_solution(12651215168413114438)
XLA Ops:
  1.3 0.0 copy-start.1
  1.3 0.7 copy-done.1
  2.0 0.0 copy-start.3
  2.0 0.1 reshape_squeeze.6
  2.1 0.6 copy-done.3
  2.7 0.1 copy.25
  2.8 0.0 copy-start
  2.8 0.1 reshape.26
  2.8 0.6 copy-done
  3.4 0.1 copy.22
  3.5 0.1 reshape_squeeze.7
  3.6 0.1 pad_add_fusion
  3.7 0.0 copy-start.4
  3.7 0.6 reshape.27.idx_ref
  4.3 0.1 copy-done.4
  4.3 0.7 %copy.24.wout_ref = bf16[128,1]{1,0:T(8,128)(2,1)} copy(bf16[128,1]{0,1:T(2,128)(2,1)S(1)} %bitcast.8) | data formatting | bytes 512 | tf_op jit(solution)/shard_map/reshape | solution.py:383
  5.1 16.7 %shard_map.175 = (f32[352,256]{1,0:T(8,128)}, f32[128,128]{1,0:T(8,128)}, f32[8,128]{1,0:T(8,128)}) custom-call(s32[1,352]{1,0:T(1,128)} %reshape.27.idx_ref, f32[3,128]{1,0:T(4,128)} %pos_ref.1, f32[128,128]{1,0:T(8,128)} %feat_ref.3, f32[128,128]{1,0:T(8,128)} %wpb_ref.3), custom_call_target="tpu_custom_call" | custom-call | tf_op jit(solution)/shard_map/pallas_call | solution.py:357
  21.8 30.3 %shard_map.176.grad_ref = f32[608,256]{1,0:T(8,128)} custom-call(s32[1]{0:T(128)S(6)} %copy.29.count_ref, s32[1,6144]{1,0:T(1,128)} %bitcast.5, s32[1,6144]{1,0:T(1,128)} %bitcast.6, f32[8,128]{1,0:T(8,128)} %get-tuple-element.9.pos_ref, f32[128,128]{1,0:T(8,128)} %feat_ref.3, f32[352,256]{1,0:T(8,128)} %get-tuple-element.10.ghost_ref, ...), custom_call_target="tpu_custom_call" | custom-call | tf_op jit(solution)/shard_map/pallas_call | solution.py:233
  52.1 13.6 %shard_map.177 = (f32[3,128]{1,0:T(4,128)}, f32[1,128]{1,0:T(1,128)}, f32[128,128]{1,0:T(8,128)}) custom-call(f32[608,256]{1,0:T(8,128)} %shard_map.176.grad_ref, s32[1,352]{1,0:T(1,128)} %reshape.27.idx_ref, f32[128,128]{1,0:T(8,128)} %wpa_ref.3, f32[128,128]{1,0:T(8,128)} %wpb_ref.3), custom_call_target="tpu_custom_call" | custom-call | tf_op jit(solution)/shard_map/pallas_call | solution.py:385
  65.7 0.0 copy-start.2
  65.7 0.7 copy-done.2
  66.4 0.0 copy-start.5
  66.4 0.6 copy.30
  66.9 0.0 copy-done.5
  67.0 0.5 copy.31
  67.5 1.5 %copy.32 = f32[128,128]{1,0:T(8,128)} copy(f32[128,128]{1,0:T(8,128)} %get-tuple-element.20) | data formatting | bytes 131072
  (2 shorter events, 0.0 us)
Async XLA Ops:
  1.3 0.7 copy-start.1
  2.0 0.7 copy-start.3
  2.8 0.7 copy-start
  3.7 0.7 copy-start.4
  65.7 0.7 copy-start.2
  66.4 0.6 copy-start.5

commit v2 on v1

v2 whole, which is shorter than its diff:
```python
import functools
import math

import jax
import jax.numpy as jnp
import numpy as np
from jax import lax
from jax.experimental import pallas as pl
from jax.experimental.pallas import tpu as pltpu
from jax.sharding import PartitionSpec as P

F32, BF16 = jnp.float32, jnp.bfloat16
MESH = pl.DeviceIdType.MESH
NN = (((1,), (0,)), ((), ()))
NT = (((1,), (1,)), ((), ()))
TN = (((0,), (0,)), ((), ()))
OWN = 128
GHOSTS = 352
ROWS = 2 * OWN + GHOSTS


def dot(a, b, dims=NN):
    return lax.dot_general(a, b, dims, preferred_element_type=F32)


def split(x, n):
    parts = []
    for _ in range(n):
        part = x.astype(BF16)
        parts.append(part)
        x = x - part.astype(F32)
    return parts


def dot32(a, b, dims=NN):
    (ah, al), (bh, bl) = split(a, 2), split(b, 2)
    return dot(ah, bh, dims) + (dot(ah, bl, dims) + dot(al, bh, dims))


def fitted(fun, degree):
    x = np.cos(np.pi * (np.arange(400) + 0.5) / 400) * 0.125 + 0.125
    series = np.polynomial.chebyshev.Chebyshev.fit(x, fun(x), degree, domain=[0, 0.25])
    return [float(v) for v in series.convert(kind=np.polynomial.Polynomial).coef]


SINE = fitted(lambda y: np.sin(2 * np.pi * np.sqrt(y)) / np.sqrt(y), 7)
COSINE = fitted(lambda y: np.cos(2 * np.pi * np.sqrt(y)), 7)


def horner(x, coefs):
    acc = coefs[-1]
    for c in coefs[-2::-1]:
        acc = acc * x + c
    return acc


def sincos_turns(t):
    f = t - jnp.round(t)
    f2 = f * f
    return f * horner(f2, SINE), horner(f2, COSINE)


def select(mask, rows):
    zero = jnp.zeros((), BF16)
    return jnp.concatenate([jnp.where(mask, r.astype(BF16), zero) for r in rows], axis=0)


def moments(mask, gv, ux, uy, uz):
    gx, gy = gv * ux, gv * uy
    return select(mask, [gv, gx, gy, gv * uz, gx * uy, gx * ux - gy * uy])


def left_operand(s, scale):
    one, x, y, z, xy, xxyy = [s[:128, 128 * j : 128 * (j + 1)] * scale for j in range(6)]
    zx, zy, zz = [s[128:, 128 * j : 128 * (j + 1)] * scale for j in (1, 2, 3)]
    k = 1.732
    e4, e5, e6, e7, e8 = (k * k) * xy, (k * k) * zy, (k * k) * zx, (k * 0.866) * xxyy, 1.5 * zz - 0.5 * one
    return jnp.concatenate(
        [
            jnp.concatenate([one - 0.5 * e8, 0.5 * x, 0.5 * y, 0.5 * z], axis=1),
            jnp.concatenate([x, e7, e4, e6], axis=1),
            jnp.concatenate([y, e4, -e7, e5], axis=1),
            jnp.concatenate([z, e6, e5, 3.0 * e8], axis=1),
        ],
        axis=0,
    ).astype(BF16)


def offset_list():
    cells = [(a, b, c) for a in (-1, 0, 1) for b in (-1, 0, 1) for c in (-1, 0, 1) if a or b or c]
    return sorted(cells, key=lambda o: abs(o[0]) + abs(o[1]) + abs(o[2]))


def blocks():
    out, start = [], 0
    for o in offset_list():
        width = (32, 8, 8)[abs(o[0]) + abs(o[1]) + abs(o[2]) - 1]
        out.append((o, start, width))
        start += width
    return out


def partner(offset, sign, sizes):
    at = [lax.axis_index(a) for a in ("gx", "gy", "gz")]
    return tuple(lax.rem(i + sign * o + n, n) for i, o, n in zip(at, offset, sizes))


def greet(sizes):
    barrier = pltpu.get_barrier_semaphore()
    for o in offset_list():
        pl.semaphore_signal(barrier, inc=1, device_id=partner(o, 1, sizes), device_id_type=MESH)


def greeted():
    pl.semaphore_wait(pltpu.get_barrier_semaphore(), 26)


def exchange(src, dst, send, recv, sign, sizes):
    copies = []
    for k, (o, start, width) in enumerate(blocks()):
        copies.append(
            pltpu.make_async_remote_copy(
                src_ref=src.at[pl.ds(start, width)],
                dst_ref=dst.at[pl.ds(start, width)],
                send_sem=send.at[k],
                recv_sem=recv.at[k],
                device_id=partner(o, sign, sizes),
                device_id_type=MESH,
            )
        )
    for copy in reversed(copies):
        copy.start()
    return copies


def lanes_to_rows(x, rows):
    x = jnp.concatenate([x, jnp.zeros((120, x.shape[1]), F32)], axis=0)
    if x.shape[1] % 128:
        x = jnp.concatenate([x, jnp.zeros((128, -x.shape[1] % 128), F32)], axis=1)
    return x.T[:rows]


def rows_to_lanes(x):
    n = x.shape[0]
    if n % 128:
        x = jnp.concatenate([x, jnp.zeros((-n % 128, 128), F32)], axis=0)
    return x.T[:, :n]


def kernel(
    sizes,
    count_ref,
    pos_ref,
    feat_ref,
    face_ref,
    edge_ref,
    corner_ref,
    centre_ref,
    other_ref,
    wpa_ref,
    wpb_ref,
    wr_ref,
    w1_ref,
    we_ref,
    wv_ref,
    w2_ref,
    wout_ref,
    force_ref,
    energy_ref,
    fgrad_ref,
    out_s,
    in_s,
    ret_s,
    oh_s,
    p_s,
    first_s,
    slope_s,
    rows_s,
    bp_s,
    send_a,
    recv_a,
    send_b,
    recv_b,
):
    edges = centre_ref.shape[1]
    greet(sizes)

    feat = feat_ref[...]
    pb = dot32(feat, wpb_ref[...])
    pos = jnp.concatenate([pos_ref[...], jnp.zeros((5, 128), F32)], axis=0)
    face, edge, corner = face_ref[0], edge_ref[0], corner_ref[0]
    pad = jnp.full((1, 6), -1, jnp.int32)
    pieces = [face[k : k + 1] for k in range(6)] + [edge[k : k + 1] for k in range(12)]
    for k in range(8):
        pieces += [corner[k : k + 1], pad]
    slots = jnp.concatenate(pieces, axis=1)
    pick = (lax.broadcasted_iota(jnp.int32, (128, GHOSTS), 0) == slots).astype(F32).astype(BF16)
    out_s[:, 0:128] = dot(pick, pb.astype(BF16), TN)
    low = dot(jnp.concatenate([p.astype(F32) for p in split(pos, 3)], axis=0).astype(BF16), pick)
    out_s[:, 128:256] = lanes_to_rows(low[0:8] + low[8:16] + low[16:24], GHOSTS)
    greeted()
    ghosts = exchange(out_s, in_s, send_a, recv_a, 1, sizes)

    iota = lax.broadcasted_iota(jnp.int32, (128, edges), 0).astype(F32).astype(BF16)
    one, zero = jnp.ones((), BF16), jnp.zeros((), BF16)
    cb = centre_ref[...].astype(F32).astype(BF16)
    o = other_ref[...]
    far = jnp.maximum(o - 416, 0)
    o = jnp.where(o < 416, o, 416 + (far >> 1) * 8 + (far & 1))
    oh_s[0:128, :] = jnp.where(iota == cb, one, zero)
    for t in range(4):
        n = 128 if t < 3 else 96
        ob = (o - 128 * t).astype(F32).astype(BF16)
        oh_s[128 * (t + 1) : 128 * (t + 1) + n, :] = jnp.where(iota[:n] == ob, one, zero)
    pa = dot32(feat, wpa_ref[...])
    table = jnp.concatenate([pa.T, pb.T], axis=1).astype(BF16)
    both = jnp.concatenate([-pos, pos], axis=1)
    places = [p.astype(F32) for p in split(both, 3)]
    places = jnp.concatenate(places + [jnp.zeros_like(both)], axis=0).astype(BF16)
    p_s[...] = dot(jnp.concatenate([table, places], axis=0), oh_s[0:256, :])
    w1 = w1_ref[...]
    w1t = w1.astype(F32).T.astype(BF16)
    wevt = jnp.concatenate([we_ref[...].astype(F32).T, wv_ref[...].astype(F32).T], axis=0).astype(BF16)
    w2 = w2_ref[...]
    w2t = w2.astype(F32).T.astype(BF16)
    wback = jnp.concatenate([w2[:128], wv_ref[...], we_ref[...]], axis=1)
    w2b = w2[128:]
    wr = wr_ref[...]
    wr_hi = wr.astype(BF16).astype(F32)
    wr_lo = wr - wr_hi
    wrt = jnp.concatenate([wr_hi, wr_lo, wr_hi, jnp.zeros((104, 128), F32)], axis=0).T[:, :32].astype(BF16)
    wr2 = jnp.concatenate([wr_hi, wr_lo], axis=0).astype(BF16)
    wout = jnp.broadcast_to(wout_ref[...].astype(F32), (128, 128)).T
    wout = jnp.concatenate([wout] * (edges // 128), axis=1)
    count = count_ref[0]

    for copy in ghosts:
        copy.wait()
    got = in_s[...]
    gpos = rows_to_lanes(got[:, 128:])[:8]
    places = [p.astype(F32) for p in split(gpos, 3)]
    places = jnp.concatenate(places + [jnp.zeros_like(gpos)], axis=0).astype(BF16)
    table = jnp.concatenate([rows_to_lanes(got[:, :128]).astype(BF16), places], axis=0)

    p = p_s[...] + dot(table, oh_s[256:ROWS, :])
    disp = p[128:136] + p[136:144] + p[144:152]
    dx, dy, dz = disp[0:1], disp[1:2], disp[2:3]
    sq = dx * dx + dy * dy + dz * dz + 0.01
    inv = lax.rsqrt(sq)
    dist = sq * inv
    ux, uy, uz = dx * inv, dy * inv, dz * inv
    is4 = 1.0 / (1.0 + 0.25 * dist * dist)
    g = is4 * is4
    gd = -dist * g * is4
    lane = lax.broadcasted_iota(jnp.int32, (1, edges), 1)
    valid = jnp.where(lane < count, 1.0, 0.0)
    gv = g * valid
    h = g * inv
    hd = (gd - h) * inv
    order = lax.broadcasted_iota(jnp.int32, (8, edges), 0).astype(F32) + 1.0
    sn, cs = sincos_turns(order * (0.25 * dist))
    basis = sn * h
    bp_s[...] = order * (math.pi / 2) * cs * h + sn * hd
    rows_s[...] = jnp.concatenate([ux, uy, uz, gv, inv, valid, gd, jnp.zeros_like(gd)], axis=0)
    b_hi = basis.astype(BF16).astype(F32)
    b4 = jnp.concatenate([b_hi, b_hi, basis - b_hi, jnp.zeros_like(basis)], axis=0).astype(BF16)
    mixed = (p[:128] + dot(wrt, b4)).astype(BF16)
    z1 = dot(w1t, mixed)
    sg = 0.5 * jnp.tanh(0.5 * z1) + 0.5
    f = z1 * sg
    first = f.astype(BF16)
    first_s[...] = first
    slope_s[...] = ((sg + f * (1.0 - sg)) * gv).astype(BF16)
    qv = dot(wevt, first)
    q, v = qv[:128].astype(BF16), qv[128:].astype(BF16)
    mask = iota == cb
    env = dot(jnp.concatenate([q, (qv[:128] * uz).astype(BF16)], axis=0), moments(mask, gv, ux, uy, uz), NT)
    left = left_operand(env, 0.2)

    m4 = select(mask, [jnp.ones_like(ux), ux, uy, uz])
    t4 = dot(left, m4)
    tx, ty, tz = t4[128:256], t4[256:384], t4[384:512]
    t = t4[:128] + (0.5 * ux) * tx + (0.5 * uy) * ty + (0.5 * uz) * tz
    vf = v.astype(F32)
    z2 = dot(w2t, jnp.concatenate([first_s[...], (vf * t).astype(BF16)], axis=0))
    sg = 0.5 * jnp.tanh(0.5 * z2) + 0.5
    f = z2 * sg
    eo = jnp.sum(f.astype(BF16).astype(F32) * wout, axis=0, keepdims=True)
    ds2 = (wout * (sg + f * (1.0 - sg))).astype(BF16)
    dsc = dot(w2b, ds2)
    dv = (t * dsc).astype(BF16)
    y = vf * dsc
    du = [jnp.sum(y * k, axis=0, keepdims=True) for k in (tx, ty, tz)]
    env = dot(jnp.concatenate([y.astype(BF16), (y * uz).astype(BF16)], axis=0), moments(mask, gv, ux, uy, uz), NT)
    left = left_operand(env, 0.2)

    d4 = dot(left, m4)
    kx, ky, kz = d4[128:256], d4[256:384], d4[384:512]
    d = d4[:128] + (0.5 * ux) * kx + (0.5 * uy) * ky + (0.5 * uz) * kz
    qf = q.astype(F32)
    du = [a + jnp.sum(qf * k, axis=0, keepdims=True) for a, k in zip(du, (kx, ky, kz))]
    dgq = jnp.sum(qf * d, axis=0, keepdims=True)
    df = dot(wback, jnp.concatenate([ds2, dv, d.astype(BF16)], axis=0))
    dz1 = (df * slope_s[...].astype(F32)).astype(BF16)
    dm = dot(w1, dz1).astype(BF16)
    db = dot(wr2, dm)
    db = db[:8] + db[8:]
    rows = rows_s[...]
    ux, uy, uz, gv = rows[0:1], rows[1:2], rows[2:3], rows[3:4]
    inv, valid, gd = rows[4:5], rows[5:6], rows[6:7]
    dux, duy, duz = [gv * a for a in du]
    dd = jnp.sum(db * bp_s[...], axis=0, keepdims=True) + valid * (eo + dgq) * gd
    dd = dd - (dux * ux + duy * uy + duz * uz) * inv
    tail = [dux * inv + dd * ux, duy * inv + dd * uy, duz * inv + dd * uz, eo * gv, jnp.zeros((4, edges), F32)]
    tail = jnp.concatenate(tail, axis=0)
    tail_hi = tail.astype(BF16).astype(F32)
    final = jnp.concatenate([dm, jnp.concatenate([tail_hi, tail - tail_hi], axis=0).astype(BF16)], axis=0)

    acc = dot(oh_s[256:ROWS, :], final, NT)
    out_s[:, 0:128] = acc[:, :128]
    out_s[:, 128:256] = jnp.concatenate([acc[:, 128:136] + acc[:, 136:144], jnp.zeros((GHOSTS, 120), F32)], axis=1)
    returns = exchange(out_s, ret_s, send_b, recv_b, -1, sizes)
    acc = dot(oh_s[0:256, :], final, NT)
    low = acc[:, 128:136] + acc[:, 136:144]
    low = jnp.concatenate([low, jnp.zeros((256, 120), F32)], axis=1).T[:8]
    part = dot32(acc[:128, :128], wpa_ref[...], NT)
    own = acc[128:, :128]
    for copy in returns:
        copy.wait()
    got = ret_s[...]
    a_hi, a_lo = split(got[:, :128], 2)
    own = own + (dot(pick, a_hi) + dot(pick, a_lo))
    back = [dot(pick, x) for x in split(got[:, 128:], 3)]
    back = (back[0] + back[1] + back[2]).T[:8]
    fgrad_ref[...] = part + dot32(own, wpb_ref[...], NT)
    force_ref[...] = low[0:3, :128] - low[0:3, 128:] - back[0:3]
    energy_ref[...] = low[3:4, :128]


def local(
    sizes,
    positions,
    atom_features,
    send_face,
    send_edge,
    send_corner,
    centre,
    other,
    edge_count,
    w_proj_a,
    w_proj_b,
    w_radial,
    w_first,
    w_env,
    w_value,
    w_second,
    w_out,
):
    vm = pl.BlockSpec(memory_space=pltpu.VMEM)
    edges = centre.shape[0]
    force, energy, fgrad = pl.pallas_call(
        functools.partial(kernel, sizes),
        out_shape=[
            jax.ShapeDtypeStruct((3, 128), F32),
            jax.ShapeDtypeStruct((1, 128), F32),
            jax.ShapeDtypeStruct((128, 128), F32),
        ],
        in_specs=[pl.BlockSpec(memory_space=pltpu.SMEM)] + [vm] * 15,
        out_specs=[vm] * 3,
        scratch_shapes=[
            pltpu.VMEM((GHOSTS, 256), F32),
            pltpu.VMEM((GHOSTS, 256), F32),
            pltpu.VMEM((GHOSTS, 256), F32),
            pltpu.VMEM((ROWS, edges), BF16),
            pltpu.VMEM((160, edges), F32),
            pltpu.VMEM((128, edges), BF16),
            pltpu.VMEM((128, edges), BF16),
            pltpu.VMEM((8, edges), F32),
            pltpu.VMEM((8, edges), F32),
        ]
        + [pltpu.SemaphoreType.DMA((26,))] * 4,
        compiler_params=pltpu.CompilerParams(
            collective_id=0, has_side_effects=True, vmem_limit_bytes=60 * 2**20
        ),
    )(
        edge_count,
        positions,
        atom_features,
        send_face,
        send_edge,
        send_corner,
        centre.reshape(1, -1),
        other.reshape(1, -1),
        w_proj_a,
        w_proj_b,
        w_radial,
        w_first,
        w_env,
        w_value,
        w_second,
        w_out.reshape(1, -1),
    )
    return force, energy.reshape(-1), fgrad


def solution(mesh):
    axes = ("gx", "gy", "gz")
    sizes = tuple(mesh.shape[a] for a in axes)
    split_first = [P(axes, None), P(axes, None, None), P(axes, None, None), P(axes, None, None)]
    return jax.shard_map(
        functools.partial(local, sizes),
        mesh=mesh,
        in_specs=(P(None, axes), *split_first, P(axes), P(axes), P(axes)) + (P(),) * 8,
        out_specs=(P(None, axes), P(axes), P(axes, None)),
        check_vma=False,
    )
```

time: 69.3 us -> 56.6 us (0.82)
  Pallas kernels: 60.6 us -> 49 us
  local copies, waits for them, and re-layouts: 6.92 us -> 5.98 us
    pallas_call x3 -> x1, Pallas kernels: 60.6 us -> 49 us  [local(): pl.pallas_call(functools.partial(kernel, sizes), out_shape=[jax.ShapeDtyp...]
    reshape x3 -> x0, local copies, waits for them, and re-layouts: 1.38 us -> none  [the longest x1 0.73 us: local(): w_out.reshape(-1, 1)]
    unnamed x17 -> x16, local copies, waits for them, and re-layouts: 5.37 us -> 5.98 us
where the time goes in v2:
time: 56.6 us; the launch traced here: 56.3 us
  Pallas kernels  49 us (87%)
  local copies, waits for them, and re-layouts  5.98 us (11%)
  between operations  1.31 us (2%)
    pallas_call x1, Pallas kernels, local(): pl.pallas_call(functools.partial(kernel, sizes), out_shape=[jax.ShapeDtyp...  49 us
    unnamed x16, local copies, waits for them, and re-layouts  5.98 us

profile of v2, /device:TPU:1, one launch (start us, length us, event | category | flops | bytes accessed | tf_op | source)
XLA Modules:
  0.0 56.3 jit_solution(8254683976766149198)
XLA Ops:
  1.3 0.0 copy-start.1
  1.3 0.7 %copy-done.1 = s32[1,6,32]{2,0,1:T(1,128)S(1)} copy-done((s32[1,6,32]{2,0,1:T(1,128)S(1)}, s32[1,6,32]{2,0,1:T(1,128)}, u32[]{:S(2)}) %copy-start.1) | copy-done | bytes 792
  2.0 0.0 copy-start.3
  2.0 0.6 %copy.19.face_ref = s32[1,6,32]{2,1,0:T(8,128)} copy(s32[1,6,32]{2,0,1:T(1,128)S(1)} %copy-done.1) | data formatting | bytes 1536 | tf_op args[2]
  2.6 0.1 copy-done.3
  2.6 0.0 copy-start
  2.6 0.7 %copy.21.corner_ref = s32[1,8,2]{2,1,0:T(8,128)} copy(s32[1,8,2]{1,2,0:T(2,128)S(1)} %copy-done.3) | data formatting | bytes 128 | tf_op args[4]
  3.3 0.0 copy-done
  3.3 0.7 %copy.20.edge_ref = s32[1,12,8]{2,1,0:T(8,128)} copy(s32[1,12,8]{1,2,0:T(8,128)S(1)} %copy-done) | data formatting | bytes 768 | tf_op args[3]
  4.0 49.0 %shard_map.175 = (f32[3,128]{1,0:T(4,128)}, f32[1,128]{1,0:T(1,128)}, f32[128,128]{1,0:T(8,128)}) custom-call(s32[1]{0:T(128)S(6)} %copy.25.count_ref, f32[3,128]{1,0:T(4,128)} %pos_ref.1, f32[128,128]{1,0:T(8,128)} %feat_ref.1, s32[1,6,32]{2,1,0:T(8,128)} %copy.19.face_ref, s32[1,12,8]{2,1,0:T(8,128)} %copy.20.edge_ref, s32[1,8,2]{2,1,0:T(8,128)} %copy.21.corner_ref, ...), custom_call_target="tpu_custom_call" | custom-call | tf_op jit(solution)/shard_map/pallas_call | solution.py:361
  53.0 0.0 copy-start.2
  53.0 0.7 %copy-done.2 = f32[3,128]{1,0:T(4,128)S(1)} copy-done((f32[3,128]{1,0:T(4,128)S(1)}, f32[3,128]{1,0:T(4,128)}, u32[]{:S(2)}) %copy-start.2) | copy-done | bytes 1560
  53.7 0.0 copy-start.4
  53.7 0.6 %copy.26 = f32[3,128]{1,0:T(4,128)} copy(f32[3,128]{1,0:T(4,128)S(1)} %copy-done.2) | data formatting | bytes 3072
  54.3 0.0 copy-done.4
  54.3 0.5 copy.27
  54.8 1.5 %copy.28 = f32[128,128]{1,0:T(8,128)} copy(f32[128,128]{1,0:T(8,128)} %get-tuple-element.14) | data formatting | bytes 131072
Async XLA Ops:
  1.3 0.7 %copy-start.1 = (s32[1,6,32]{2,0,1:T(1,128)S(1)}, s32[1,6,32]{2,0,1:T(1,128)}, u32[]{:S(2)}) copy-start(s32[1,6,32]{2,0,1:T(1,128)} %param.18) | copy-start | bytes 2308
  2.0 0.7 %copy-start.3 = (s32[1,8,2]{1,2,0:T(2,128)S(1)}, s32[1,8,2]{1,2,0:T(2,128)}, u32[]{:S(2)}) copy-start(s32[1,8,2]{1,2,0:T(2,128)} %param.20) | copy-start | bytes 196
  2.6 0.7 %copy-start = (s32[1,12,8]{1,2,0:T(8,128)S(1)}, s32[1,12,8]{1,2,0:T(8,128)}, u32[]{:S(2)}) copy-start(s32[1,12,8]{1,2,0:T(8,128)} %param.19) | copy-start | bytes 1156
  53.0 0.7 %copy-start.2 = (f32[3,128]{1,0:T(4,128)S(1)}, f32[3,128]{1,0:T(4,128)}, u32[]{:S(2)}) copy-start(f32[3,128]{1,0:T(4,128)} %get-tuple-element.12) | copy-start | bytes 4612
  53.7 0.6 %copy-start.4 = (f32[1,128]{1,0:T(1,128)S(1)}, f32[1,128]{1,0:T(1,128)}, u32[]{:S(2)}) copy-start(f32[1,128]{1,0:T(1,128)} %get-tuple-element.7) | copy-start | bytes 1540

commit v3 on v2

--- a/solution.py
+++ b/solution.py
@@ -17,6 +17,7 @@
 OWN = 128
 GHOSTS = 352
 ROWS = 2 * OWN + GHOSTS
+WIDTH = 1024
 
 
 def dot(a, b, dims=NN):
@@ -145,6 +146,27 @@
     if n % 128:
         x = jnp.concatenate([x, jnp.zeros((-n % 128, 128), F32)], axis=0)
     return x.T[:, :n]
+
+
+def staggered(make, count):
+    live = []
+    for k in range(count):
+        live.append(make(k))
+        live = [x for x in live if advance(x)]
+    while live:
+        live = [x for x in live if advance(x)]
+
+
+def advance(x):
+    try:
+        next(x)
+    except StopIteration:
+        return False
+    return True
+
+
+def total(parts):
+    return functools.reduce(jnp.add, parts)
 
 
 def kernel(
@@ -165,8 +187,7 @@
     wv_ref,
     w2_ref,
     wout_ref,
-    force_ref,
-    energy_ref,
+    small_ref,
     fgrad_ref,
     out_s,
     in_s,
@@ -175,6 +196,12 @@
     p_s,
     first_s,
     slope_s,
+    q_s,
+    v_s,
+    ds2_s,
+    dv_s,
+    final_s,
+    saved_s,
     rows_s,
     bp_s,
     send_a,
@@ -183,16 +210,20 @@
     recv_b,
 ):
     edges = centre_ref.shape[1]
+    width = WIDTH
     greet(sizes)
 
     feat = feat_ref[...]
-    pb = dot32(feat, wpb_ref[...])
+    w1 = w1_ref[...]
+    w1b = sum(dot(x, w1) for x in split(wpb_ref[...], 3))
+    pb = dot32(feat, w1b)
     pos = jnp.concatenate([pos_ref[...], jnp.zeros((5, 128), F32)], axis=0)
-    face, edge, corner = face_ref[0], edge_ref[0], corner_ref[0]
-    pad = jnp.full((1, 6), -1, jnp.int32)
-    pieces = [face[k : k + 1] for k in range(6)] + [edge[k : k + 1] for k in range(12)]
-    for k in range(8):
-        pieces += [corner[k : k + 1], pad]
+    edge = jnp.concatenate([edge_ref[0].astype(F32), jnp.zeros((8, 116), F32)], axis=1)
+    corner = jnp.concatenate([corner_ref[0].astype(F32), jnp.full((6, 8), -1.0, F32)], axis=0)
+    corner = jnp.concatenate([corner, jnp.zeros((8, 120), F32)], axis=1)
+    lists = jnp.concatenate([edge, corner, jnp.zeros((112, 128), F32)], axis=0).T.astype(jnp.int32)
+    pieces = [face_ref[k] for k in range(6)] + [lists[k : k + 1, 0:8] for k in range(12)]
+    pieces += [lists[k : k + 1, 8:16] for k in range(8)]
     slots = jnp.concatenate(pieces, axis=1)
     pick = (lax.broadcasted_iota(jnp.int32, (128, GHOSTS), 0) == slots).astype(F32).astype(BF16)
     out_s[:, 0:128] = dot(pick, pb.astype(BF16), TN)
@@ -212,20 +243,19 @@
         n = 128 if t < 3 else 96
         ob = (o - 128 * t).astype(F32).astype(BF16)
         oh_s[128 * (t + 1) : 128 * (t + 1) + n, :] = jnp.where(iota[:n] == ob, one, zero)
-    pa = dot32(feat, wpa_ref[...])
+    w1a = sum(dot(x, w1) for x in split(wpa_ref[...], 3))
+    pa = dot32(feat, w1a)
     table = jnp.concatenate([pa.T, pb.T], axis=1).astype(BF16)
     both = jnp.concatenate([-pos, pos], axis=1)
     places = [p.astype(F32) for p in split(both, 3)]
     places = jnp.concatenate(places + [jnp.zeros_like(both)], axis=0).astype(BF16)
     p_s[...] = dot(jnp.concatenate([table, places], axis=0), oh_s[0:256, :])
-    w1 = w1_ref[...]
-    w1t = w1.astype(F32).T.astype(BF16)
     wevt = jnp.concatenate([we_ref[...].astype(F32).T, wv_ref[...].astype(F32).T], axis=0).astype(BF16)
     w2 = w2_ref[...]
     w2t = w2.astype(F32).T.astype(BF16)
     wback = jnp.concatenate([w2[:128], wv_ref[...], we_ref[...]], axis=1)
     w2b = w2[128:]
-    wr = wr_ref[...]
+    wr = sum(dot(x, w1) for x in split(jnp.concatenate([wr_ref[...], jnp.zeros((8, 128), F32)], axis=0), 3))[:8]
     wr_hi = wr.astype(BF16).astype(F32)
     wr_lo = wr - wr_hi
     wrt = jnp.concatenate([wr_hi, wr_lo, wr_hi, jnp.zeros((104, 128), F32)], axis=0).T[:, :32].astype(BF16)
@@ -242,88 +272,125 @@
     places = jnp.concatenate(places + [jnp.zeros_like(gpos)], axis=0).astype(BF16)
     table = jnp.concatenate([rows_to_lanes(got[:, :128]).astype(BF16), places], axis=0)
 
-    p = p_s[...] + dot(table, oh_s[256:ROWS, :])
-    disp = p[128:136] + p[136:144] + p[144:152]
-    dx, dy, dz = disp[0:1], disp[1:2], disp[2:3]
-    sq = dx * dx + dy * dy + dz * dz + 0.01
-    inv = lax.rsqrt(sq)
-    dist = sq * inv
-    ux, uy, uz = dx * inv, dy * inv, dz * inv
-    is4 = 1.0 / (1.0 + 0.25 * dist * dist)
-    g = is4 * is4
-    gd = -dist * g * is4
-    lane = lax.broadcasted_iota(jnp.int32, (1, edges), 1)
-    valid = jnp.where(lane < count, 1.0, 0.0)
-    gv = g * valid
-    h = g * inv
-    hd = (gd - h) * inv
-    order = lax.broadcasted_iota(jnp.int32, (8, edges), 0).astype(F32) + 1.0
-    sn, cs = sincos_turns(order * (0.25 * dist))
-    basis = sn * h
-    bp_s[...] = order * (math.pi / 2) * cs * h + sn * hd
-    rows_s[...] = jnp.concatenate([ux, uy, uz, gv, inv, valid, gd, jnp.zeros_like(gd)], axis=0)
-    b_hi = basis.astype(BF16).astype(F32)
-    b4 = jnp.concatenate([b_hi, b_hi, basis - b_hi, jnp.zeros_like(basis)], axis=0).astype(BF16)
-    mixed = (p[:128] + dot(wrt, b4)).astype(BF16)
-    z1 = dot(w1t, mixed)
-    sg = 0.5 * jnp.tanh(0.5 * z1) + 0.5
-    f = z1 * sg
-    first = f.astype(BF16)
-    first_s[...] = first
-    slope_s[...] = ((sg + f * (1.0 - sg)) * gv).astype(BF16)
-    qv = dot(wevt, first)
-    q, v = qv[:128].astype(BF16), qv[128:].astype(BF16)
-    mask = iota == cb
-    env = dot(jnp.concatenate([q, (qv[:128] * uz).astype(BF16)], axis=0), moments(mask, gv, ux, uy, uz), NT)
-    left = left_operand(env, 0.2)
-
-    m4 = select(mask, [jnp.ones_like(ux), ux, uy, uz])
-    t4 = dot(left, m4)
-    tx, ty, tz = t4[128:256], t4[256:384], t4[384:512]
-    t = t4[:128] + (0.5 * ux) * tx + (0.5 * uy) * ty + (0.5 * uz) * tz
-    vf = v.astype(F32)
-    z2 = dot(w2t, jnp.concatenate([first_s[...], (vf * t).astype(BF16)], axis=0))
-    sg = 0.5 * jnp.tanh(0.5 * z2) + 0.5
-    f = z2 * sg
-    eo = jnp.sum(f.astype(BF16).astype(F32) * wout, axis=0, keepdims=True)
-    ds2 = (wout * (sg + f * (1.0 - sg))).astype(BF16)
-    dsc = dot(w2b, ds2)
-    dv = (t * dsc).astype(BF16)
-    y = vf * dsc
-    du = [jnp.sum(y * k, axis=0, keepdims=True) for k in (tx, ty, tz)]
-    env = dot(jnp.concatenate([y.astype(BF16), (y * uz).astype(BF16)], axis=0), moments(mask, gv, ux, uy, uz), NT)
-    left = left_operand(env, 0.2)
-
-    d4 = dot(left, m4)
-    kx, ky, kz = d4[128:256], d4[256:384], d4[384:512]
-    d = d4[:128] + (0.5 * ux) * kx + (0.5 * uy) * ky + (0.5 * uz) * kz
-    qf = q.astype(F32)
-    du = [a + jnp.sum(qf * k, axis=0, keepdims=True) for a, k in zip(du, (kx, ky, kz))]
-    dgq = jnp.sum(qf * d, axis=0, keepdims=True)
-    df = dot(wback, jnp.concatenate([ds2, dv, d.astype(BF16)], axis=0))
-    dz1 = (df * slope_s[...].astype(F32)).astype(BF16)
-    dm = dot(w1, dz1).astype(BF16)
-    db = dot(wr2, dm)
-    db = db[:8] + db[8:]
-    rows = rows_s[...]
-    ux, uy, uz, gv = rows[0:1], rows[1:2], rows[2:3], rows[3:4]
-    inv, valid, gd = rows[4:5], rows[5:6], rows[6:7]
-    dux, duy, duz = [gv * a for a in du]
-    dd = jnp.sum(db * bp_s[...], axis=0, keepdims=True) + valid * (eo + dgq) * gd
-    dd = dd - (dux * ux + duy * uy + duz * uz) * inv
-    tail = [dux * inv + dd * ux, duy * inv + dd * uy, duz * inv + dd * uz, eo * gv, jnp.zeros((4, edges), F32)]
-    tail = jnp.concatenate(tail, axis=0)
-    tail_hi = tail.astype(BF16).astype(F32)
-    final = jnp.concatenate([dm, jnp.concatenate([tail_hi, tail - tail_hi], axis=0).astype(BF16)], axis=0)
-
-    acc = dot(oh_s[256:ROWS, :], final, NT)
+    def group(k):
+        at = slice(k * width, (k + 1) * width)
+        cols = pl.ds(k * width, width)
+
+        p = p_s[:, cols] + dot(table, oh_s[256:ROWS, cols])
+        yield
+        disp = p[128:136] + p[136:144] + p[144:152]
+        dx, dy, dz = disp[0:1], disp[1:2], disp[2:3]
+        sq = dx * dx + dy * dy + dz * dz + 0.01
+        inv = lax.rsqrt(sq)
+        dist = sq * inv
+        ux, uy, uz = dx * inv, dy * inv, dz * inv
+        is4 = 1.0 / (1.0 + 0.25 * dist * dist)
+        g = is4 * is4
+        gd = -dist * g * is4
+        lane = lax.broadcasted_iota(jnp.int32, (1, width), 1) + k * width
+        valid = jnp.where(lane < count, 1.0, 0.0)
+        gv = g * valid
+        h = g * inv
+        hd = (gd - h) * inv
+        order = lax.broadcasted_iota(jnp.int32, (8, width), 0).astype(F32) + 1.0
+        sn, cs = sincos_turns(order * (0.25 * dist))
+        basis = sn * h
+        bp_s[:, cols] = order * (math.pi / 2) * cs * h + sn * hd
+        rows_s[:, cols] = jnp.concatenate([ux, uy, uz, gv, inv, valid, gd, jnp.zeros_like(gd)], axis=0)
+        b_hi = basis.astype(BF16).astype(F32)
+        b4 = jnp.concatenate([b_hi, b_hi, basis - b_hi, jnp.zeros_like(basis)], axis=0).astype(BF16)
+        z1 = p[:128] + dot(wrt, b4)
+        yield
+        sg = 0.5 * jnp.tanh(0.5 * z1) + 0.5
+        f = z1 * sg
+        first = f.astype(BF16)
+        first_s[:, cols] = first
+        slope_s[:, cols] = ((sg + f * (1.0 - sg)) * gv).astype(BF16)
+        qv = dot(wevt, first)
+        yield
+        q_s[:, cols] = qv[:128].astype(BF16)
+        v_s[:, cols] = qv[128:].astype(BF16)
+        mask = iota[:, at] == cb[:, at]
+        pair = jnp.concatenate([qv[:128].astype(BF16), (qv[:128] * uz).astype(BF16)], axis=0)
+        env.append(dot(pair, moments(mask, gv, ux, uy, uz), NT))
+
+    def group_b(k):
+        at = slice(k * width, (k + 1) * width)
+        cols = pl.ds(k * width, width)
+        rows = rows_s[:, cols]
+        ux, uy, uz, gv = rows[0:1], rows[1:2], rows[2:3], rows[3:4]
+        mask = iota[:, at] == cb[:, at]
+        t4 = dot(left, select(mask, [jnp.ones_like(ux), ux, uy, uz]))
+        yield
+        tx, ty, tz = t4[128:256], t4[256:384], t4[384:512]
+        t = t4[:128] + (0.5 * ux) * tx + (0.5 * uy) * ty + (0.5 * uz) * tz
+        vf = v_s[:, cols].astype(F32)
+        z2 = dot(w2t, jnp.concatenate([first_s[:, cols], (vf * t).astype(BF16)], axis=0))
+        yield
+        sg = 0.5 * jnp.tanh(0.5 * z2) + 0.5
+        f = z2 * sg
+        eo = jnp.sum(f.astype(BF16).astype(F32) * wout[:, at], axis=0, keepdims=True)
+        ds2 = (wout[:, at] * (sg + f * (1.0 - sg))).astype(BF16)
+        ds2_s[:, cols] = ds2
+        dsc = dot(w2b, ds2)
+        yield
+        dv_s[:, cols] = (t * dsc).astype(BF16)
+        y = vf * dsc
+        du = [jnp.sum(y * c, axis=0, keepdims=True) for c in (tx, ty, tz)]
+        saved_s[:, cols] = jnp.concatenate(du + [eo, jnp.zeros((4, width), F32)], axis=0)
+        pair = jnp.concatenate([y.astype(BF16), (y * uz).astype(BF16)], axis=0)
+        env.append(dot(pair, moments(mask, gv, ux, uy, uz), NT))
+
+    def group_c(k):
+        at = slice(k * width, (k + 1) * width)
+        cols = pl.ds(k * width, width)
+        rows = rows_s[:, cols]
+        ux, uy, uz, gv = rows[0:1], rows[1:2], rows[2:3], rows[3:4]
+        mask = iota[:, at] == cb[:, at]
+        d4 = dot(left, select(mask, [jnp.ones_like(ux), ux, uy, uz]))
+        yield
+        kx, ky, kz = d4[128:256], d4[256:384], d4[384:512]
+        d = d4[:128] + (0.5 * ux) * kx + (0.5 * uy) * ky + (0.5 * uz) * kz
+        qf = q_s[:, cols].astype(F32)
+        saved = saved_s[:, cols]
+        dux, duy, duz = [saved[j : j + 1] + jnp.sum(qf * c, axis=0, keepdims=True) for j, c in enumerate((kx, ky, kz))]
+        dgq = jnp.sum(qf * d, axis=0, keepdims=True)
+        df = dot(wback, jnp.concatenate([ds2_s[:, cols], dv_s[:, cols], d.astype(BF16)], axis=0))
+        yield
+        dz1 = (df * slope_s[:, cols].astype(F32)).astype(BF16)
+        db = dot(wr2, dz1)
+        yield
+        db = db[:8] + db[8:]
+        inv, valid, gd = rows[4:5], rows[5:6], rows[6:7]
+        dux, duy, duz = gv * dux, gv * duy, gv * duz
+        eo = saved[3:4]
+        dd = jnp.sum(db * bp_s[:, cols], axis=0, keepdims=True) + valid * (eo + dgq) * gd
+        dd = dd - (dux * ux + duy * uy + duz * uz) * inv
+        tail = [dux * inv + dd * ux, duy * inv + dd * uy, duz * inv + dd * uz, eo * gv, jnp.zeros((4, width), F32)]
+        tail = jnp.concatenate(tail, axis=0)
+        tail_hi = tail.astype(BF16).astype(F32)
+        low = jnp.concatenate([tail_hi, tail - tail_hi], axis=0).astype(BF16)
+        final = jnp.concatenate([dz1, low], axis=0)
+        final_s[:, cols] = final
+        env.append(dot(oh_s[256:ROWS, cols], final, NT))
+
+    env = []
+    staggered(group, edges // width)
+    left = left_operand(total(env), 0.2)
+    env = []
+    staggered(group_b, edges // width)
+    left = left_operand(total(env), 0.2)
+    env = []
+    staggered(group_c, edges // width)
+
+    acc = total(env)
     out_s[:, 0:128] = acc[:, :128]
     out_s[:, 128:256] = jnp.concatenate([acc[:, 128:136] + acc[:, 136:144], jnp.zeros((GHOSTS, 120), F32)], axis=1)
     returns = exchange(out_s, ret_s, send_b, recv_b, -1, sizes)
-    acc = dot(oh_s[0:256, :], final, NT)
+    acc = dot(oh_s[0:256, :], final_s[...], NT)
     low = acc[:, 128:136] + acc[:, 136:144]
     low = jnp.concatenate([low, jnp.zeros((256, 120), F32)], axis=1).T[:8]
-    part = dot32(acc[:128, :128], wpa_ref[...], NT)
+    part = dot32(acc[:128, :128], w1a, NT)
     own = acc[128:, :128]
     for copy in returns:
         copy.wait()
@@ -332,9 +399,14 @@
     own = own + (dot(pick, a_hi) + dot(pick, a_lo))
     back = [dot(pick, x) for x in split(got[:, 128:], 3)]
     back = (back[0] + back[1] + back[2]).T[:8]
-    fgrad_ref[...] = part + dot32(own, wpb_ref[...], NT)
-    force_ref[...] = low[0:3, :128] - low[0:3, 128:] - back[0:3]
-    energy_ref[...] = low[3:4, :128]
+    fgrad_ref[...] = part + dot32(own, w1b, NT)
+    small_ref[...] = jnp.concatenate([low[0:3, :128] - low[0:3, 128:] - back[0:3], low[3:8, :128]], axis=0)
+
+
+def place(small_ref, wide_ref, force_ref, energy_ref, fgrad_ref):
+    force_ref[...] = small_ref[0:3, :]
+    energy_ref[...] = small_ref[3:4, :]
+    fgrad_ref[...] = wide_ref[...]
 
 
 def local(
@@ -358,23 +430,20 @@
 ):
     vm = pl.BlockSpec(memory_space=pltpu.VMEM)
     edges = centre.shape[0]
-    force, energy, fgrad = pl.pallas_call(
+    small, wide = pl.pallas_call(
         functools.partial(kernel, sizes),
-        out_shape=[
-            jax.ShapeDtypeStruct((3, 128), F32),
-            jax.ShapeDtypeStruct((1, 128), F32),
-            jax.ShapeDtypeStruct((128, 128), F32),
-        ],
+        out_shape=[jax.ShapeDtypeStruct((8, 128), F32), jax.ShapeDtypeStruct((128, 128), F32)],
         in_specs=[pl.BlockSpec(memory_space=pltpu.SMEM)] + [vm] * 15,
-        out_specs=[vm] * 3,
+        out_specs=[vm] * 2,
         scratch_shapes=[
             pltpu.VMEM((GHOSTS, 256), F32),
             pltpu.VMEM((GHOSTS, 256), F32),
             pltpu.VMEM((GHOSTS, 256), F32),
             pltpu.VMEM((ROWS, edges), BF16),
             pltpu.VMEM((160, edges), F32),
-            pltpu.VMEM((128, edges), BF16),
-            pltpu.VMEM((128, edges), BF16),
+            *[pltpu.VMEM((128, edges), BF16)] * 6,
+            pltpu.VMEM((144, edges), BF16),
+            pltpu.VMEM((8, edges), F32),
             pltpu.VMEM((8, edges), F32),
             pltpu.VMEM((8, edges), F32),
         ]
@@ -386,9 +455,9 @@
         edge_count,
         positions,
         atom_features,
-        send_face,
-        send_edge,
-        send_corner,
+        jnp.transpose(send_face, (1, 0, 2)),
+        jnp.transpose(send_edge, (0, 2, 1)),
+        jnp.transpose(send_corner, (0, 2, 1)),
         centre.reshape(1, -1),
         other.reshape(1, -1),
         w_proj_a,
@@ -400,6 +469,16 @@
         w_second,
         w_out.reshape(1, -1),
     )
+    force, energy, fgrad = pl.pallas_call(
+        place,
+        out_shape=[
+            jax.ShapeDtypeStruct((3, 128), F32),
+            jax.ShapeDtypeStruct((1, 128), F32),
+            jax.ShapeDtypeStruct((128, 128), F32),
+        ],
+        in_specs=[vm] * 2,
+        out_specs=[vm] * 3,
+    )(small, wide)
     return force, energy.reshape(-1), fgrad
 
 

time: 56.6 us -> 49.2 us (0.87)
  local copies, waits for them, and re-layouts: 5.98 us -> 0 us
  Pallas kernels: 49 us -> 47.6 us
    unnamed x16 -> x0, local copies, waits for them, and re-layouts: 5.98 us -> none
    pallas_call x1, Pallas kernels: 49 us -> 46.2 us  [local(): pl.pallas_call(functools.partial(kernel, sizes), out_shape=[jax.ShapeDtyp...]
    pallas_call x0 -> x1, Pallas kernels: none -> 1.49 us  [local(): pl.pallas_call(place, out_shape=[jax.ShapeDtypeStruct((3, 128), F32), jax...]
where the time goes in v3:
time: 49.2 us; the launch traced here: 48.9 us
  Pallas kernels  47.6 us (97%)
  between operations  1.29 us (3%)
    pallas_call x1, Pallas kernels, local(): pl.pallas_call(functools.partial(kernel, sizes), out_shape=[jax.ShapeDtyp...  46.2 us
    pallas_call x1, Pallas kernels, local(): pl.pallas_call(place, out_shape=[jax.ShapeDtypeStruct((3, 128), F32), jax...  1.49 us

profile of v3, /device:TPU:1, one launch (start us, length us, event | category | flops | bytes accessed | tf_op | source)
XLA Modules:
  0.0 48.9 jit_solution(10891841853638401810)
XLA Ops:
  1.3 46.2 %shard_map.175 = (f32[8,128]{1,0:T(8,128)}, f32[128,128]{1,0:T(8,128)}) custom-call(s32[1]{0:T(128)S(6)} %copy.19.count_ref, f32[3,128]{1,0:T(4,128)} %pos_ref.1, f32[128,128]{1,0:T(8,128)} %feat_ref.1, s32[6,1,32]{2,1,0:T(1,128)} %bitcast.10, s32[1,8,12]{2,1,0:T(8,128)} %bitcast.9, s32[1,2,8]{2,1,0:T(2,128)} %bitcast.11, s32[1,6144]{1,0:T(1,128)} %bitcast.7, ...), custom_call_target="tpu_custom_call" | custom-call | tf_op jit(solution)/shard_map/pallas_call | solution.py:433
  47.4 1.5 %shard_map.176 = (f32[3,128]{1,0:T(4,128)}, f32[1,128]{1,0:T(1,128)}, f32[128,128]{1,0:T(8,128)}) custom-call(f32[8,128]{1,0:T(8,128)} %get-tuple-element.8.small_ref, f32[128,128]{1,0:T(8,128)} %get-tuple-element.9.wide_ref), custom_call_target="tpu_custom_call" | custom-call | tf_op jit(solution)/shard_map/pallas_call | solution.py:472

commit v4 on v3

--- a/solution.py
+++ b/solution.py
@@ -117,21 +117,19 @@
 
 
 def exchange(src, dst, send, recv, sign, sizes):
-    copies = []
-    for k, (o, start, width) in enumerate(blocks()):
-        copies.append(
-            pltpu.make_async_remote_copy(
-                src_ref=src.at[pl.ds(start, width)],
-                dst_ref=dst.at[pl.ds(start, width)],
-                send_sem=send.at[k],
-                recv_sem=recv.at[k],
-                device_id=partner(o, sign, sizes),
-                device_id_type=MESH,
-            )
+    def copy(rows, offset):
+        return pltpu.make_async_remote_copy(
+            src_ref=src.at[rows],
+            dst_ref=dst.at[rows],
+            send_sem=send,
+            recv_sem=recv,
+            device_id=partner(offset, sign, sizes),
+            device_id_type=MESH,
         )
-    for copy in reversed(copies):
-        copy.start()
-    return copies
+
+    for offset, start, rows in reversed(blocks()):
+        copy(pl.ds(start, rows), offset).start()
+    return copy(pl.ds(0, GHOSTS), blocks()[0][0])
 
 
 def lanes_to_rows(x, rows):
@@ -172,6 +170,23 @@
 def kernel(
     sizes,
     count_ref,
+    pos_hbm,
+    feat_hbm,
+    face_hbm,
+    edge_hbm,
+    corner_hbm,
+    centre_hbm,
+    other_hbm,
+    wpa_hbm,
+    wpb_hbm,
+    wr_hbm,
+    w1_hbm,
+    we_hbm,
+    wv_hbm,
+    w2_hbm,
+    wout_ref,
+    small_ref,
+    fgrad_ref,
     pos_ref,
     feat_ref,
     face_ref,
@@ -186,9 +201,6 @@
     we_ref,
     wv_ref,
     w2_ref,
-    wout_ref,
-    small_ref,
-    fgrad_ref,
     out_s,
     in_s,
     ret_s,
@@ -202,16 +214,41 @@
     dv_s,
     final_s,
     saved_s,
+    acc_s,
     rows_s,
     bp_s,
     send_a,
     recv_a,
     send_b,
     recv_b,
+    load,
 ):
     edges = centre_ref.shape[1]
     width = WIDTH
+    pairs = [
+        (feat_hbm, feat_ref),
+        (wpb_hbm, wpb_ref),
+        (w1_hbm, w1_ref),
+        (pos_hbm, pos_ref),
+        (face_hbm, face_ref),
+        (edge_hbm, edge_ref),
+        (corner_hbm, corner_ref),
+        (centre_hbm, centre_ref),
+        (other_hbm, other_ref),
+        (wpa_hbm, wpa_ref),
+        (wr_hbm, wr_ref),
+        (we_hbm, we_ref),
+        (wv_hbm, wv_ref),
+        (w2_hbm, w2_ref),
+    ]
+    loads = [pltpu.make_async_copy(src, dst, load.at[k]) for k, (src, dst) in enumerate(pairs)]
+    for copy in loads[:7]:
+        copy.start()
     greet(sizes)
+    for copy in loads[7:]:
+        copy.start()
+    for copy in loads[:7]:
+        copy.wait()
 
     feat = feat_ref[...]
     w1 = w1_ref[...]
@@ -231,6 +268,8 @@
     out_s[:, 128:256] = lanes_to_rows(low[0:8] + low[8:16] + low[16:24], GHOSTS)
     greeted()
     ghosts = exchange(out_s, in_s, send_a, recv_a, 1, sizes)
+    for copy in loads[7:]:
+        copy.wait()
 
     iota = lax.broadcasted_iota(jnp.int32, (128, edges), 0).astype(F32).astype(BF16)
     one, zero = jnp.ones((), BF16), jnp.zeros((), BF16)
@@ -264,8 +303,7 @@
     wout = jnp.concatenate([wout] * (edges // 128), axis=1)
     count = count_ref[0]
 
-    for copy in ghosts:
-        copy.wait()
+    ghosts.wait()
     got = in_s[...]
     gpos = rows_to_lanes(got[:, 128:])[:8]
     places = [p.astype(F32) for p in split(gpos, 3)]
@@ -387,13 +425,20 @@
     out_s[:, 0:128] = acc[:, :128]
     out_s[:, 128:256] = jnp.concatenate([acc[:, 128:136] + acc[:, 136:144], jnp.zeros((GHOSTS, 120), F32)], axis=1)
     returns = exchange(out_s, ret_s, send_b, recv_b, -1, sizes)
-    acc = dot(oh_s[0:256, :], final_s[...], NT)
+    acc_s[...] = jnp.zeros_like(acc_s)
+
+    def owned(k, carry):
+        cols = pl.ds(pl.multiple_of(k * (edges // 2), 128), edges // 2)
+        acc_s[...] += dot(oh_s[0:256, cols], final_s[:, cols], NT)
+        return carry
+
+    lax.fori_loop(0, 2, owned, 0)
+    acc = acc_s[...]
     low = acc[:, 128:136] + acc[:, 136:144]
     low = jnp.concatenate([low, jnp.zeros((256, 120), F32)], axis=1).T[:8]
     part = dot32(acc[:128, :128], w1a, NT)
     own = acc[128:, :128]
-    for copy in returns:
-        copy.wait()
+    returns.wait()
     got = ret_s[...]
     a_hi, a_lo = split(got[:, :128], 2)
     own = own + (dot(pick, a_hi) + dot(pick, a_lo))
@@ -430,29 +475,7 @@
 ):
     vm = pl.BlockSpec(memory_space=pltpu.VMEM)
     edges = centre.shape[0]
-    small, wide = pl.pallas_call(
-        functools.partial(kernel, sizes),
-        out_shape=[jax.ShapeDtypeStruct((8, 128), F32), jax.ShapeDtypeStruct((128, 128), F32)],
-        in_specs=[pl.BlockSpec(memory_space=pltpu.SMEM)] + [vm] * 15,
-        out_specs=[vm] * 2,
-        scratch_shapes=[
-            pltpu.VMEM((GHOSTS, 256), F32),
-            pltpu.VMEM((GHOSTS, 256), F32),
-            pltpu.VMEM((GHOSTS, 256), F32),
-            pltpu.VMEM((ROWS, edges), BF16),
-            pltpu.VMEM((160, edges), F32),
-            *[pltpu.VMEM((128, edges), BF16)] * 6,
-            pltpu.VMEM((144, edges), BF16),
-            pltpu.VMEM((8, edges), F32),
-            pltpu.VMEM((8, edges), F32),
-            pltpu.VMEM((8, edges), F32),
-        ]
-        + [pltpu.SemaphoreType.DMA((26,))] * 4,
-        compiler_params=pltpu.CompilerParams(
-            collective_id=0, has_side_effects=True, vmem_limit_bytes=60 * 2**20
-        ),
-    )(
-        edge_count,
+    operands = [
         positions,
         atom_features,
         jnp.transpose(send_face, (1, 0, 2)),
@@ -468,7 +491,32 @@
         w_value,
         w_second,
         w_out.reshape(1, -1),
-    )
+    ]
+    small, wide = pl.pallas_call(
+        functools.partial(kernel, sizes),
+        out_shape=[jax.ShapeDtypeStruct((8, 128), F32), jax.ShapeDtypeStruct((128, 128), F32)],
+        in_specs=[pl.BlockSpec(memory_space=pltpu.SMEM)] + [pl.BlockSpec(memory_space=pl.ANY)] * 14 + [vm],
+        out_specs=[vm] * 2,
+        scratch_shapes=[pltpu.VMEM(x.shape, x.dtype) for x in operands[:14]]
+        + [
+            pltpu.VMEM((GHOSTS, 256), F32),
+            pltpu.VMEM((GHOSTS, 256), F32),
+            pltpu.VMEM((GHOSTS, 256), F32),
+            pltpu.VMEM((ROWS, edges), BF16),
+            pltpu.VMEM((160, edges), F32),
+            *[pltpu.VMEM((128, edges), BF16)] * 6,
+            pltpu.VMEM((144, edges), BF16),
+            pltpu.VMEM((8, edges), F32),
+            pltpu.VMEM((256, 144), F32),
+            pltpu.VMEM((8, edges), F32),
+            pltpu.VMEM((8, edges), F32),
+        ]
+        + [pltpu.SemaphoreType.DMA(())] * 4
+        + [pltpu.SemaphoreType.DMA((14,))],
+        compiler_params=pltpu.CompilerParams(
+            collective_id=0, has_side_effects=True, vmem_limit_bytes=60 * 2**20
+        ),
+    )(edge_count, *operands)
     force, energy, fgrad = pl.pallas_call(
         place,
         out_shape=[

time: 49.2 us -> 48.3 us (0.982)
  Pallas kernels: 47.6 us -> 46.8 us
    pallas_call x1, Pallas kernels: 46.2 us -> 45.3 us  [local(): pl.pallas_call(functools.partial(kernel, sizes), out_shape=[jax.ShapeDtyp...]
where the time goes in v4:
time: 48.3 us; the launch traced here: 48.1 us
  Pallas kernels  46.8 us (97%)
  between operations  1.29 us (3%)
    pallas_call x1, Pallas kernels, local(): pl.pallas_call(functools.partial(kernel, sizes), out_shape=[jax.ShapeDtyp...  45.3 us
    pallas_call x1, Pallas kernels, local(): pl.pallas_call(place, out_shape=[jax.ShapeDtypeStruct((3, 128), F32), jax...  1.49 us

profile of v4, /device:TPU:1, one launch (start us, length us, event | category | flops | bytes accessed | tf_op | source)
XLA Modules:
  0.0 48.1 jit_solution(7483964769249478801)
XLA Ops:
  1.3 45.3 %shard_map.175 = (f32[8,128]{1,0:T(8,128)}, f32[128,128]{1,0:T(8,128)}) custom-call(s32[1]{0:T(128)S(6)} %copy.19.count_ref, f32[3,128]{1,0:T(4,128)} %pos_hbm.1, f32[128,128]{1,0:T(8,128)} %feat_hbm.1, s32[6,1,32]{2,1,0:T(1,128)} %bitcast.10, s32[1,8,12]{2,1,0:T(8,128)} %bitcast.9, s32[1,2,8]{2,1,0:T(2,128)} %bitcast.11, s32[1,6144]{1,0:T(1,128)} %bitcast.7, ...), custom_call_target="tpu_custom_call" | custom-call | tf_op jit(solution)/shard_map/pallas_call | solution.py:495
  46.6 1.5 %shard_map.176 = (f32[3,128]{1,0:T(4,128)}, f32[1,128]{1,0:T(1,128)}, f32[128,128]{1,0:T(8,128)}) custom-call(f32[8,128]{1,0:T(8,128)} %get-tuple-element.8.small_ref, f32[128,128]{1,0:T(8,128)} %get-tuple-element.9.wide_ref), custom_call_target="tpu_custom_call" | custom-call | tf_op jit(solution)/shard_map/pallas_call | solution.py:520

commit v5 on v4

--- a/solution.py
+++ b/solution.py
@@ -17,7 +17,7 @@
 OWN = 128
 GHOSTS = 352
 ROWS = 2 * OWN + GHOSTS
-WIDTH = 1024
+WIDTHS = (512, 1024, 1024, 1024, 1024, 1024, 512)
 
 
 def dot(a, b, dims=NN):
@@ -146,10 +146,11 @@
     return x.T[:, :n]
 
 
-def staggered(make, count):
-    live = []
-    for k in range(count):
-        live.append(make(k))
+def staggered(make, widths):
+    live, start = [], 0
+    for width in widths:
+        live.append(make(start, width))
+        start += width
         live = [x for x in live if advance(x)]
     while live:
         live = [x for x in live if advance(x)]
@@ -224,7 +225,6 @@
     load,
 ):
     edges = centre_ref.shape[1]
-    width = WIDTH
     pairs = [
         (feat_hbm, feat_ref),
         (wpb_hbm, wpb_ref),
@@ -310,9 +310,9 @@
     places = jnp.concatenate(places + [jnp.zeros_like(gpos)], axis=0).astype(BF16)
     table = jnp.concatenate([rows_to_lanes(got[:, :128]).astype(BF16), places], axis=0)
 
-    def group(k):
-        at = slice(k * width, (k + 1) * width)
-        cols = pl.ds(k * width, width)
+    def group(start, width):
+        at = slice(start, start + width)
+        cols = pl.ds(start, width)
 
         p = p_s[:, cols] + dot(table, oh_s[256:ROWS, cols])
         yield
@@ -325,7 +325,7 @@
         is4 = 1.0 / (1.0 + 0.25 * dist * dist)
         g = is4 * is4
         gd = -dist * g * is4
-        lane = lax.broadcasted_iota(jnp.int32, (1, width), 1) + k * width
+        lane = lax.broadcasted_iota(jnp.int32, (1, width), 1) + start
         valid = jnp.where(lane < count, 1.0, 0.0)
         gv = g * valid
         h = g * inv
@@ -352,9 +352,9 @@
         pair = jnp.concatenate([qv[:128].astype(BF16), (qv[:128] * uz).astype(BF16)], axis=0)
         env.append(dot(pair, moments(mask, gv, ux, uy, uz), NT))
 
-    def group_b(k):
-        at = slice(k * width, (k + 1) * width)
-        cols = pl.ds(k * width, width)
+    def group_b(start, width):
+        at = slice(start, start + width)
+        cols = pl.ds(start, width)
         rows = rows_s[:, cols]
         ux, uy, uz, gv = rows[0:1], rows[1:2], rows[2:3], rows[3:4]
         mask = iota[:, at] == cb[:, at]
@@ -379,9 +379,9 @@
         pair = jnp.concatenate([y.astype(BF16), (y * uz).astype(BF16)], axis=0)
         env.append(dot(pair, moments(mask, gv, ux, uy, uz), NT))
 
-    def group_c(k):
-        at = slice(k * width, (k + 1) * width)
-        cols = pl.ds(k * width, width)
+    def group_c(start, width):
+        at = slice(start, start + width)
+        cols = pl.ds(start, width)
         rows = rows_s[:, cols]
         ux, uy, uz, gv = rows[0:1], rows[1:2], rows[2:3], rows[3:4]
         mask = iota[:, at] == cb[:, at]
@@ -413,13 +413,13 @@
         env.append(dot(oh_s[256:ROWS, cols], final, NT))
 
     env = []
-    staggered(group, edges // width)
+    staggered(group, WIDTHS)
     left = left_operand(total(env), 0.2)
     env = []
-    staggered(group_b, edges // width)
+    staggered(group_b, WIDTHS)
     left = left_operand(total(env), 0.2)
     env = []
-    staggered(group_c, edges // width)
+    staggered(group_c, WIDTHS)
 
     acc = total(env)
     out_s[:, 0:128] = acc[:, :128]
@@ -494,7 +494,7 @@
     ]
     small, wide = pl.pallas_call(
         functools.partial(kernel, sizes),
-        out_shape=[jax.ShapeDtypeStruct((8, 128), F32), jax.ShapeDtypeStruct((128, 128), F32)],
+        out_shape=[pltpu.VMEM((8, 128), F32), pltpu.VMEM((128, 128), F32)],
         in_specs=[pl.BlockSpec(memory_space=pltpu.SMEM)] + [pl.BlockSpec(memory_space=pl.ANY)] * 14 + [vm],
         out_specs=[vm] * 2,
         scratch_shapes=[pltpu.VMEM(x.shape, x.dtype) for x in operands[:14]]
@@ -514,7 +514,7 @@
         + [pltpu.SemaphoreType.DMA(())] * 4
         + [pltpu.SemaphoreType.DMA((14,))],
         compiler_params=pltpu.CompilerParams(
-            collective_id=0, has_side_effects=True, vmem_limit_bytes=60 * 2**20
+            collective_id=0, has_side_effects=True, vmem_limit_bytes=56 * 2**20
         ),
     )(edge_count, *operands)
     force, energy, fgrad = pl.pallas_call(
@@ -526,7 +526,7 @@
         ],
         in_specs=[vm] * 2,
         out_specs=[vm] * 3,
-    )(small, wide)
+    )(*[pltpu.with_memory_space_constraint(x, pltpu.VMEM) for x in (small, wide)])
     return force, energy.reshape(-1), fgrad
 
 

time: 48.3 us -> 46.3 us (0.959)
  Pallas kernels: 46.8 us -> 44.8 us
    pallas_call x1, Pallas kernels: 45.3 us -> 44.2 us  [local(): pl.pallas_call(functools.partial(kernel, sizes), out_shape=[pltpu.VMEM((8...]
    pallas_call x1, Pallas kernels: 1.49 us -> 0.64 us  [local(): pl.pallas_call(place, out_shape=[jax.ShapeDtypeStruct((3, 128), F32), jax...]
where the time goes in v5:
time: 46.3 us; the launch traced here: 46.1 us
  Pallas kernels  44.8 us (97%)
  between operations  1.29 us (3%)
    pallas_call x1, Pallas kernels, local(): pl.pallas_call(functools.partial(kernel, sizes), out_shape=[pltpu.VMEM((8...  44.2 us

profile of v5, /device:TPU:1, one launch (start us, length us, event | category | flops | bytes accessed | tf_op | source)
XLA Modules:
  0.0 46.1 jit_solution(11866204449127597569)
XLA Ops:
  1.3 44.2 %shard_map.175 = (f32[8,128]{1,0:T(8,128)S(1)}, f32[128,128]{1,0:T(8,128)S(1)}) custom-call(s32[1]{0:T(128)S(6)} %copy.19.count_ref, f32[3,128]{1,0:T(4,128)} %pos_hbm.1, f32[128,128]{1,0:T(8,128)} %feat_hbm.1, s32[6,1,32]{2,1,0:T(1,128)} %bitcast.10, s32[1,8,12]{2,1,0:T(8,128)} %bitcast.9, s32[1,2,8]{2,1,0:T(2,128)} %bitcast.11, s32[1,6144]{1,0:T(1,128)} %bitcast.7, ...), custom_call_target="tpu_custom_call" | custom-call | tf_op jit(solution)/shard_map/pallas_call | solution.py:495
  45.4 0.6 %shard_map.176 = (f32[3,128]{1,0:T(4,128)}, f32[1,128]{1,0:T(1,128)}, f32[128,128]{1,0:T(8,128)}) custom-call(f32[8,128]{1,0:T(8,128)S(1)} %get-tuple-element.8.small_ref, f32[128,128]{1,0:T(8,128)S(1)} %get-tuple-element.9.wide_ref), custom_call_target="tpu_custom_call" | custom-call | tf_op jit(solution)/shard_map/pallas_call | solution.py:520

commit v6 on v5

--- a/solution.py
+++ b/solution.py
@@ -17,7 +17,7 @@
 OWN = 128
 GHOSTS = 352
 ROWS = 2 * OWN + GHOSTS
-WIDTHS = (512, 1024, 1024, 1024, 1024, 1024, 512)
+WIDTHS = (256, 768, 1024, 1024, 1024, 1024, 768, 256)
 
 
 def dot(a, b, dims=NN):
@@ -149,11 +149,15 @@
 def staggered(make, widths):
     live, start = [], 0
     for width in widths:
-        live.append(make(start, width))
+        live.insert(0, make(start, width))
         start += width
         live = [x for x in live if advance(x)]
     while live:
         live = [x for x in live if advance(x)]
+
+
+def ranges(widths):
+    return [pl.ds(sum(widths[:k]), width) for k, width in enumerate(widths)]
 
 
 def advance(x):
@@ -289,10 +293,12 @@
     places = [p.astype(F32) for p in split(both, 3)]
     places = jnp.concatenate(places + [jnp.zeros_like(both)], axis=0).astype(BF16)
     p_s[...] = dot(jnp.concatenate([table, places], axis=0), oh_s[0:256, :])
-    wevt = jnp.concatenate([we_ref[...].astype(F32).T, wv_ref[...].astype(F32).T], axis=0).astype(BF16)
+    we = we_ref[...]
+    wet = we.astype(F32).T.astype(BF16)
+    wvt = wv_ref[...].astype(F32).T.astype(BF16)
     w2 = w2_ref[...]
     w2t = w2.astype(F32).T.astype(BF16)
-    wback = jnp.concatenate([w2[:128], wv_ref[...], we_ref[...]], axis=1)
+    wback = jnp.concatenate([w2[:128], wv_ref[...]], axis=1)
     w2b = w2[128:]
     wr = sum(dot(x, w1) for x in split(jnp.concatenate([wr_ref[...], jnp.zeros((8, 128), F32)], axis=0), 3))[:8]
     wr_hi = wr.astype(BF16).astype(F32)
@@ -344,12 +350,11 @@
         first = f.astype(BF16)
         first_s[:, cols] = first
         slope_s[:, cols] = ((sg + f * (1.0 - sg)) * gv).astype(BF16)
-        qv = dot(wevt, first)
-        yield
-        q_s[:, cols] = qv[:128].astype(BF16)
-        v_s[:, cols] = qv[128:].astype(BF16)
+        q = dot(wet, first)
+        yield
+        q_s[:, cols] = q.astype(BF16)
         mask = iota[:, at] == cb[:, at]
-        pair = jnp.concatenate([qv[:128].astype(BF16), (qv[:128] * uz).astype(BF16)], axis=0)
+        pair = jnp.concatenate([q.astype(BF16), (q * uz).astype(BF16)], axis=0)
         env.append(dot(pair, moments(mask, gv, ux, uy, uz), NT))
 
     def group_b(start, width):
@@ -393,7 +398,7 @@
         saved = saved_s[:, cols]
         dux, duy, duz = [saved[j : j + 1] + jnp.sum(qf * c, axis=0, keepdims=True) for j, c in enumerate((kx, ky, kz))]
         dgq = jnp.sum(qf * d, axis=0, keepdims=True)
-        df = dot(wback, jnp.concatenate([ds2_s[:, cols], dv_s[:, cols], d.astype(BF16)], axis=0))
+        df = p_s[0:128, cols] + dot(we, d.astype(BF16))
         yield
         dz1 = (df * slope_s[:, cols].astype(F32)).astype(BF16)
         db = dot(wr2, dz1)
@@ -414,9 +419,13 @@
 
     env = []
     staggered(group, WIDTHS)
+    for cols in ranges(WIDTHS):
+        v_s[:, cols] = dot(wvt, first_s[:, cols]).astype(BF16)
     left = left_operand(total(env), 0.2)
     env = []
     staggered(group_b, WIDTHS)
+    for cols in ranges(WIDTHS):
+        p_s[0:128, cols] = dot(wback, jnp.concatenate([ds2_s[:, cols], dv_s[:, cols]], axis=0))
     left = left_operand(total(env), 0.2)
     env = []
     staggered(group_c, WIDTHS)

time: 46.3 us -> 45.8 us (0.989)
  Pallas kernels: 44.8 us -> 44.3 us
    pallas_call x1, Pallas kernels: 44.2 us -> 43.7 us  [local(): pl.pallas_call(functools.partial(kernel, sizes), out_shape=[pltpu.VMEM((8...]
where the time goes in v6:
time: 45.8 us; the launch traced here: 45.6 us
  Pallas kernels  44.3 us (97%)
  between operations  1.29 us (3%)
    pallas_call x1, Pallas kernels, local(): pl.pallas_call(functools.partial(kernel, sizes), out_shape=[pltpu.VMEM((8...  43.7 us

profile of v6, /device:TPU:1, one launch (start us, length us, event | category | flops | bytes accessed | tf_op | source)
XLA Modules:
  0.0 45.6 jit_solution(3617897661218910899)
XLA Ops:
  1.3 43.7 %shard_map.175 = (f32[8,128]{1,0:T(8,128)S(1)}, f32[128,128]{1,0:T(8,128)S(1)}) custom-call(s32[1]{0:T(128)S(6)} %copy.19.count_ref, f32[3,128]{1,0:T(4,128)} %pos_hbm.1, f32[128,128]{1,0:T(8,128)} %feat_hbm.1, s32[6,1,32]{2,1,0:T(1,128)} %bitcast.10, s32[1,8,12]{2,1,0:T(8,128)} %bitcast.9, s32[1,2,8]{2,1,0:T(2,128)} %bitcast.11, s32[1,6144]{1,0:T(1,128)} %bitcast.7, ...), custom_call_target="tpu_custom_call" | custom-call | tf_op jit(solution)/shard_map/pallas_call | solution.py:504
  45.0 0.6 %shard_map.176 = (f32[3,128]{1,0:T(4,128)}, f32[1,128]{1,0:T(1,128)}, f32[128,128]{1,0:T(8,128)}) custom-call(f32[8,128]{1,0:T(8,128)S(1)} %get-tuple-element.8.small_ref, f32[128,128]{1,0:T(8,128)S(1)} %get-tuple-element.9.wide_ref), custom_call_target="tpu_custom_call" | custom-call | tf_op jit(solution)/shard_map/pallas_call | solution.py:529
